TPU v7x, 512 devices: a whole 4x8x8 slice. The times are simulated.
512 devices in a mesh: slab: 128 (over y, x, z_lo), row: 4 (over z_hi, core).
Axes of the slice: x: 4, y: 8, z: 8 (z_hi: 2, z_lo: 4; z = z_hi * 4 + z_lo), core: 2. Of those that a mesh axis runs over, the one named last changes fastest.
Arguments:
- volume: bfloat16 [128, 2048, 2048], P('row', 'slab'), may hold values from -3 to 3
- magnify: float32 [128], P('row'), as said below
- goal: float32 [2048, 2048], P('slab', 'row'), may hold values from -6 to 6
- live_pixels: int32 [2048, 2048], P('slab', 'row'), may hold values 0 or 1
Outputs:
- projection: float32 [2048, 2048], P('slab', 'row')
- backprojection: bfloat16 [128, 2048, 2048], P('row', 'slab')
Inputs may be any that keep to these rules, and one draw needn't show every extreme that they name: magnify rises strictly with the plane index and lies between 1 - s and 1 + s with s = 29 / 1025.
All inputs are finite; a program needn't handle non-finite values. No bound on the sum of `live_pixels` on one device may be relied on, other than what follows from the above.
Results may differ from a plain program's by a relative error of at most 0.009.
Values may be sent and summed in bfloat16 or wider, within the bound.
No kernel may reach another device: no remote copies, remote signals or barrier semaphores. Data moves between devices by JAX's collectives and lax.ppermute only.
A program may use at most 64 MiB of HBM per device.

v0:
```python
import math

import jax
import jax.numpy as jnp
from jax import lax
from jax.sharding import PartitionSpec as P

REACH = 2
BLOCKS = 5


def shifted(block, axis, distance):
    devices = range(lax.axis_size(axis))
    route = [(i - distance, i) for i in devices if i - distance in devices]
    return lax.ppermute(block, axis, route)


def hat_columns(factor, width, block_count, reach_cols, cols_det, cols_vol):
    span = (2 * reach_cols + 1) * width
    block_ids = jnp.arange(block_count, dtype=jnp.int32)
    columns = (block_ids[:, None] * width + jnp.arange(width, dtype=jnp.int32)[None, :]).astype(
        jnp.float32
    )
    samples = (columns + 0.5 - cols_det / 2) / factor + (cols_vol / 2 - 0.5)
    source = (
        (block_ids[:, None] - reach_cols) * width + jnp.arange(span, dtype=jnp.int32)[None, :]
    ).astype(jnp.float32)
    valid = (source >= 0.0) & (source < cols_vol)
    weights = jnp.maximum(0.0, 1.0 - jnp.abs(samples[:, None, :] - source[:, :, None]))
    return jnp.where(valid[:, :, None], weights, 0.0).astype(jnp.bfloat16)


def hat_rows(factor, det_first, vol_first, frame_rows, slab_rows, rows_all):
    detector = (det_first + jnp.arange(frame_rows, dtype=jnp.int32)).astype(jnp.float32)
    samples = (detector + 0.5 - rows_all / 2) / factor + (rows_all / 2 - 0.5)
    source = (vol_first + jnp.arange(slab_rows, dtype=jnp.int32)).astype(jnp.float32)
    return jnp.maximum(0.0, 1.0 - jnp.abs(samples[:, None] - source[None, :])).astype(jnp.bfloat16)


def collect(blocks):
    summed = blocks[REACH]
    for position in range(BLOCKS):
        if position != REACH:
            summed = summed + shifted(
                blocks[position].astype(jnp.bfloat16), "slab", position - REACH
            ).astype(jnp.float32)
    return summed


def spread(owned):
    pieces = {REACH: owned}
    for position in range(BLOCKS):
        if position != REACH:
            pieces[position] = shifted(owned, "slab", REACH - position)
    return jnp.stack([pieces[position] for position in range(BLOCKS)])


def shards(volume, magnify, goal, live_pixels):
    planes, slab_rows, cols_vol = volume.shape
    own_rows, own_cols = goal.shape
    row_count = lax.axis_size("row")
    cols_det = own_cols * row_count
    rows_all = slab_rows * lax.axis_size("slab")
    frame_rows = BLOCKS * slab_rows
    width = min(128, cols_det)
    block_count = cols_det // width
    spread_bound = (REACH * slab_rows - 3.0) / (rows_all / 2.0 + 1.0)
    shift_bound = cols_det / 2.0 * (1.0 / (1.0 - spread_bound) - 1.0) + 2.0
    reach_cols = max(1, int(math.ceil(shift_bound / width)))
    span_blocks = 2 * reach_cols + 1
    slab_index = lax.axis_index("slab")
    vol_first = slab_index * slab_rows
    det_first = (slab_index - REACH) * slab_rows

    def forward_plane(inputs):
        slice_data, factor = inputs
        weights = hat_columns(factor, width, block_count, reach_cols, cols_det, cols_vol)
        blocked = slice_data.reshape(slab_rows, block_count, width)
        padded = jnp.pad(blocked, ((0, 0), (reach_cols, reach_cols), (0, 0)))
        windows = jnp.concatenate(
            [padded[:, shift_pos : shift_pos + block_count] for shift_pos in range(span_blocks)],
            axis=2,
        )
        pieces = jnp.einsum("zbw,bwc->zbc", windows, weights, preferred_element_type=jnp.float32)
        resampled = pieces.reshape(slab_rows, cols_det).astype(jnp.bfloat16)
        row_weights = hat_rows(factor, det_first, vol_first, frame_rows, slab_rows, rows_all)
        return (resampled, row_weights)

    resampled_all, row_weights_all = lax.map(forward_plane, (volume, magnify))
    frame = lax.dot_general(
        row_weights_all,
        resampled_all,
        (((0, 2), (0, 1)), ((), ())),
        preferred_element_type=jnp.float32,
    )
    projection = lax.psum_scatter(
        collect(frame.reshape(BLOCKS, slab_rows, cols_det)), "row", scatter_dimension=1, tiled=True
    )
    residual = ((projection - goal) * live_pixels.astype(jnp.float32)).astype(jnp.bfloat16)
    frame_res = spread(lax.all_gather(residual, "row", axis=1, tiled=True)).reshape(
        frame_rows, cols_det
    )

    def backward_plane(inputs):
        factor, row_weights = inputs
        weights = hat_columns(factor, width, block_count, reach_cols, cols_det, cols_vol)
        smeared = lax.dot_general(
            row_weights, frame_res, (((0,), (0,)), ((), ())), preferred_element_type=jnp.float32
        ).astype(jnp.bfloat16)
        split_cols = smeared.reshape(slab_rows, block_count, width)
        pieces = jnp.einsum("zbc,bwc->zbw", split_cols, weights, preferred_element_type=jnp.float32)
        pieces = pieces.reshape(slab_rows, block_count, span_blocks, width)
        summed = jnp.zeros((slab_rows, block_count + 2 * reach_cols, width), jnp.float32)
        for shift_pos in range(span_blocks):
            summed = summed + jnp.pad(
                pieces[:, :, shift_pos], ((0, 0), (shift_pos, span_blocks - 1 - shift_pos), (0, 0))
            )
        kept = summed[:, reach_cols : reach_cols + block_count]
        return kept.reshape(slab_rows, cols_vol).astype(jnp.bfloat16)

    backprojection = lax.map(backward_plane, (magnify, row_weights_all))
    return (projection, backprojection)


def solution(mesh):
    in_specs = (P("row", "slab", None), P("row"), P("slab", "row"), P("slab", "row"))
    out_specs = (P("slab", "row"), P("row", "slab", None))
    return jax.shard_map(shards, mesh=mesh, in_specs=in_specs, out_specs=out_specs, check_vma=False)
```

profile of v0, /device:TPU:57, one launch (start us, length us, event | category | flops | bytes accessed | tf_op | source)
XLA Modules:
  0.0 536.0 jit_solution(11916733982830375866)
XLA Ops:
  7.8 198.7 %while.31 = (s32[]{:T(128)}, bf16[32,16,2048]{2,1,0:T(8,128)(2,1)S(1)}, bf16[32,80,16]{1,2,0:T(8,128)(2,1)S(1)}, f32[32]{0:T(128)S(1)}, bf16[32,16,2048]{2,1,0:T(8,128)(2,1)}, /*index=5*/s32[]{:T(128)}, s32[]{:T(128)}, s32[]{:T(128)}) while((s32[]{:T(128)}, bf16[32,16,2048]{2,1,0:T(8,128)(2,1)S(1)}, bf16[32,80,16]{1,2,0:T(8,128)(2,1)S(1)}, ...), condition=%wide.region_1.2_spmd, body=%wide.region_0.1_spmd.sunk | while | flops 30567136 | bytes 1328957 | solution.py:89
  16.3 3.1 fusion.45
  41.2 3.1 fusion.45
  59.8 3.1 fusion.45
  66.0 3.1 fusion.45
  84.6 3.1 fusion.45
  90.8 3.1 fusion.45
  109.5 3.1 fusion.45
  207.0 8.8 %collective-permute-start = (bf16[16,2048]{1,0:T(8,128)(2,1)S(1)}, bf16[16,2048]{1,0:T(8,128)(2,1)S(1)}, u32[]{:S(2)}, u32[]{:S(2)}) collective-permute-start(bf16[16,2048]{1,0:T(8,128)(2,1)S(1)} %get-tuple-element.311), channel_id=1, source_target_pairs={{8,0},{12,4},{16,8},{20,12},{24,16},{28,20},{32,24},{36,28},{40,32... | collective-permute-start | bytes 196616 | tf_op jit(solution)/shard_map/ppermute | solution.py:15
  215.8 3.7 collective-permute-start.1
  224.9 4.5 collective-permute-done.2
  232.0 41.8 %reduce-scatter.2.cloned.1.call-done = f32[16,512]{1,0:T(8,128)} async-done(((f32[16,2048]{1,0:T(8,128)}), f32[16,512]{1,0:T(8,128)}) %reduce-scatter.2.cloned.1.call-update) | async-done | bytes 32784 | tf_op jit(solution)/shard_map/reduce_scatter | solution.py:96
  274.6 9.6 %all_gather.3 = bf16[16,2048]{1,0:T(8,128)(2,1)S(1)} all-gather(bf16[16,512]{1,0:T(8,128)(2,1)S(1)} %multiply_convert_fusion), channel_id=1, replica_groups=mesh['slab'=128,'row'=4] {'row'}, dimensions={1}, use_global_device_ids=true | all-gather | bytes 81920 | tf_op jit(solution)/shard_map/all_gather | solution.py:100
  289.0 7.5 %collective-permute-start.6 = (bf16[16,2048]{1,0:T(8,128)(2,1)S(1)}, bf16[16,2048]{1,0:T(8,128)(2,1)S(1)}, u32[]{:S(2)}, u32[]{:S(2)}) collective-permute-start(bf16[16,2048]{1,0:T(8,128)(2,1)S(1)} %all_gather.3), channel_id=1, source_target_pairs={{4,0},{8,4},{12,8},{16,12},{20,16},{24,20},{28,24},{32,28},{36,32}... | collective-permute-start | bytes 196616 | tf_op jit(solution)/shard_map/ppermute | solution.py:15
  298.8 3.6 collective-permute-done.7
  302.7 225.2 %while.32 = (s32[]{:T(128)}, bf16[32,16,2048]{2,1,0:T(8,128)(2,1)S(1)}, f32[32]{0:T(128)S(1)}, bf16[32,80,16]{1,2,0:T(8,128)(2,1)S(1)}, bf16[80,2048]{1,0:T(8,128)(2,1)S(1)}, /*index=5*/s32[]{:T(128)}) while((s32[]{:T(128)}, bf16[32,16,2048]{2,1,0:T(8,128)(2,1)S(1)}, f32[32]{0:T(128)S(1)}, bf16[32,80,16]{1,2,0:T(8,128)(2,1)S(1)}, ...), condition=%wide.region_4.5_spmd, body=%wide.region_3.4_spmd.sunk | while | flops 35311664 | bytes 4014493 | solution.py:121
  304.4 4.7 fusion.51
  311.4 4.7 fusion.51
  318.4 4.7 fusion.51
  325.5 4.7 fusion.51
  332.5 4.7 fusion.51
  339.5 4.7 fusion.51
  346.6 4.7 fusion.51
  353.6 4.7 fusion.51
  360.6 4.7 fusion.51
  367.7 4.7 fusion.51
  374.7 4.7 fusion.51
  381.8 4.7 fusion.51
  388.8 4.7 fusion.51
  395.8 4.7 fusion.51
  402.9 4.7 fusion.51
  409.9 4.7 fusion.51
  416.9 4.7 fusion.51
  424.0 4.7 fusion.51
  431.0 4.7 fusion.51
  438.0 4.7 fusion.51
  445.1 4.7 fusion.51
  452.1 4.7 fusion.51
  459.2 4.7 fusion.51
  466.2 4.7 fusion.51
  473.2 4.7 fusion.51
  480.3 4.7 fusion.51
  487.3 4.7 fusion.51
  494.3 4.7 fusion.51
  501.4 4.7 fusion.51
  508.4 4.7 fusion.51
  515.4 4.7 fusion.51
  522.5 4.7 fusion.51
  (986 shorter events, 265.8 us)
Async XLA Ops:
  7.2 0.7 copy-start.3
  7.2 266.6 %reduce-scatter.2.cloned.1.call-start = ((), (), s32[]{:S(2)}) async-start(), calls=%async_computation.1 | async-start | bytes 163840 | tf_op jit(solution)/shard_map/reduce_scatter | solution.py:96
  206.5 67.4 %copy-start.1 = (s32[16,512]{1,0:T(8,128)S(1)}, s32[16,512]{1,0:T(8,128)}, u32[]{:S(2)}) copy-start(s32[16,512]{1,0:T(8,128)} %param.11) | copy-start | bytes 98308
  206.5 67.4 %copy-start.2 = (f32[16,512]{1,0:T(8,128)S(1)}, f32[16,512]{1,0:T(8,128)}, u32[]{:S(2)}) copy-start(f32[16,512]{1,0:T(8,128)} %param.10) | copy-start | bytes 98308
  207.0 17.8 %collective-permute-start = (bf16[16,2048]{1,0:T(8,128)(2,1)S(1)}, bf16[16,2048]{1,0:T(8,128)(2,1)S(1)}, u32[]{:S(2)}, u32[]{:S(2)}) collective-permute-start(bf16[16,2048]{1,0:T(8,128)(2,1)S(1)} %get-tuple-element.311), channel_id=1, source_target_pairs={{8,0},{12,4},{16,8},{20,12},{24,16},{28,20},{32,24},{36,28},{40,32... | collective-permute-start | bytes 196616 | tf_op jit(solution)/shard_map/ppermute | solution.py:15
  215.8 9.0 %collective-permute-start.1 = (bf16[16,2048]{1,0:T(8,128)(2,1)S(1)}, bf16[16,2048]{1,0:T(8,128)(2,1)S(1)}, u32[]{:S(2)}, u32[]{:S(2)}) collective-permute-start(bf16[16,2048]{1,0:T(8,128)(2,1)S(1)} %get-tuple-element.314), channel_id=1, source_target_pairs={{4,0},{8,4},{12,8},{16,12},{20,16},{24,20},{28,24},{32,28},{36,32}... | collective-permute-start | bytes 196616 | tf_op jit(solution)/shard_map/ppermute | solution.py:15
  219.6 9.8 %collective-permute-start.2 = (bf16[16,2048]{1,0:T(8,128)(2,1)S(1)}, bf16[16,2048]{1,0:T(8,128)(2,1)S(1)}, u32[]{:S(2)}, u32[]{:S(2)}) collective-permute-start(bf16[16,2048]{1,0:T(8,128)(2,1)S(1)} %get-tuple-element.313), channel_id=1, source_target_pairs={{0,4},{4,8},{8,12},{12,16},{16,20},{20,24},{24,28},{28,32},{32,36}... | collective-permute-start | bytes 196616 | tf_op jit(solution)/shard_map/ppermute | solution.py:15
  221.8 9.5 %collective-permute-start.3 = (bf16[16,2048]{1,0:T(8,128)(2,1)S(1)}, bf16[16,2048]{1,0:T(8,128)(2,1)S(1)}, u32[]{:S(2)}, u32[]{:S(2)}) collective-permute-start(bf16[16,2048]{1,0:T(8,128)(2,1)S(1)} %get-tuple-element.312), channel_id=1, source_target_pairs={{0,8},{4,12},{8,16},{12,20},{16,24},{20,28},{24,32},{28,36},{32,40... | collective-permute-start | bytes 196616 | tf_op jit(solution)/shard_map/ppermute | solution.py:15
  284.2 14.5 %collective-permute-start.4 = (bf16[16,2048]{1,0:T(8,128)(2,1)S(1)}, bf16[16,2048]{1,0:T(8,128)(2,1)S(1)}, u32[]{:S(2)}, u32[]{:S(2)}) collective-permute-start(bf16[16,2048]{1,0:T(8,128)(2,1)S(1)} %all_gather.3), channel_id=1, source_target_pairs={{0,8},{4,12},{8,16},{12,20},{16,24},{20,28},{24,32},{28,36},{32,40... | collective-permute-start | bytes 196616 | tf_op jit(solution)/shard_map/ppermute | solution.py:15
  286.4 12.3 %collective-permute-start.5 = (bf16[16,2048]{1,0:T(8,128)(2,1)S(1)}, bf16[16,2048]{1,0:T(8,128)(2,1)S(1)}, u32[]{:S(2)}, u32[]{:S(2)}) collective-permute-start(bf16[16,2048]{1,0:T(8,128)(2,1)S(1)} %all_gather.3), channel_id=1, source_target_pairs={{0,4},{4,8},{8,12},{12,16},{16,20},{20,24},{24,28},{28,32},{32,36}... | collective-permute-start | bytes 196616 | tf_op jit(solution)/shard_map/ppermute | solution.py:15
  289.0 9.8 %collective-permute-start.6 = (bf16[16,2048]{1,0:T(8,128)(2,1)S(1)}, bf16[16,2048]{1,0:T(8,128)(2,1)S(1)}, u32[]{:S(2)}, u32[]{:S(2)}) collective-permute-start(bf16[16,2048]{1,0:T(8,128)(2,1)S(1)} %all_gather.3), channel_id=1, source_target_pairs={{4,0},{8,4},{12,8},{16,12},{20,16},{24,20},{28,24},{32,28},{36,32}... | collective-permute-start | bytes 196616 | tf_op jit(solution)/shard_map/ppermute | solution.py:15
  296.5 5.9 %collective-permute-start.7 = (bf16[16,2048]{1,0:T(8,128)(2,1)S(1)}, bf16[16,2048]{1,0:T(8,128)(2,1)S(1)}, u32[]{:S(2)}, u32[]{:S(2)}) collective-permute-start(bf16[16,2048]{1,0:T(8,128)(2,1)S(1)} %all_gather.3), channel_id=1, source_target_pairs={{8,0},{12,4},{16,8},{20,12},{24,16},{28,20},{32,24},{36,28},{40,32... | collective-permute-start | bytes 196616 | tf_op jit(solution)/shard_map/ppermute | solution.py:15
  527.9 1.3 copy-start
Sparse Core Ops, SparseCore 0:
  232.1 41.6 reduce-scatter.1
where the time goes:
time: 542 us; the launch traced here: 536 us
  matrix products  256 us (47%)
  local copies, waits for them, and re-layouts  90.3 us (17%)
  other arithmetic  77.3 us (14%)
  waiting for transfers between devices  51.9 us (10%)
  starting transfers between devices  32.3 us (6%)
  between operations  14.2 us (3%)
  blocking collectives  9.65 us (2%)
    dot_general x32, matrix products, backward_plane(): jnp.einsum('zbc,bwc->zbw', split_cols, weights, preferred_element_type=jn...  150 us
    dot_general x32, matrix products, forward_plane(): jnp.einsum('zbw,bwc->zbc', windows, weights, preferred_element_type=jnp.f...  100 us
    add x64, other arithmetic, hat_columns(): samples = (columns + 0.5 - cols_det / 2) / factor + (cols_vol / 2 - 0.5)  43.1 us
    reduce_scatter x1, waiting for transfers between devices, shards(): lax.psum_scatter(collect(frame.reshape(BLOCKS, slab_rows, cols_det)), 'ro...  41.8 us
    dynamic_slice x64, local copies, waits for them, and re-layouts, shards(): resampled_all, row_weights_all = lax.map(forward_plane, (volume, magnify))  37.8 us
    ppermute x8, starting transfers between devices, shifted(): return lax.ppermute(block, axis, route)  32.3 us
    while x64, local copies, waits for them, and re-layouts  27.5 us
    add x32, other arithmetic, hat_rows(): samples = (detector + 0.5 - rows_all / 2) / factor + (rows_all / 2 - 0.5)  18.1 us
  transfers between devices with their start and end apart: 9, of which 4 were waited for; matrix products, arithmetic and copies ran while one was open for 0% of the time, Pallas kernels for 0%

commit v1 on v0

v1 whole, which is shorter than its diff:
```python
import functools

import jax
import jax.numpy as jnp
from jax import lax
from jax.experimental import pallas as pl
from jax.experimental.pallas import tpu as pltpu
from jax.sharding import PartitionSpec as P

REACH = 2
BLOCKS = 2 * REACH + 1
LANES = 128
GROUP = 8
MARGIN = 32
DEAD = 1e30

LANE_GATHER = lax.GatherDimensionNumbers(
    offset_dims=(),
    collapsed_slice_dims=(1,),
    start_index_map=(1,),
    operand_batching_dims=(0,),
    start_indices_batching_dims=(0,),
)


def pick(block, lanes):
    return lax.gather(
        block,
        lanes[..., None],
        LANE_GATHER,
        (1, 1),
        mode=lax.GatherScatterMode.PROMISE_IN_BOUNDS,
    )


def pick_two(first, second, where_from):
    lanes = where_from & (LANES - 1)
    return jnp.where(where_from >= LANES, pick(second, lanes), pick(first, lanes))


def shifted(block, axis, distance):
    devices = range(lax.axis_size(axis))
    route = [(i - distance, i) for i in devices if i - distance in devices]
    return lax.ppermute(block, axis, route)


def factors_on_sublanes(magnify_ref, first):
    plane = lax.broadcasted_iota(jnp.int32, (GROUP, LANES), 0)
    factors = jnp.full((GROUP, LANES), magnify_ref[first], jnp.float32)
    for i in range(1, GROUP):
        factors = jnp.where(plane == i, magnify_ref[first + i], factors)
    return factors


def rounded(weights):
    return weights.astype(jnp.bfloat16).astype(jnp.float32)


def forward_kernel(
    place_ref, magnify_ref, volume_ref, own_ref, m2_ref, m1_ref, p1_ref, p2_ref,
    resampled, row_table, source, low, high,
):
    group = pl.program_id(0)
    first = group * GROUP
    slab_rows = volume_ref.shape[1]
    cols = volume_ref.shape[2]
    half = cols // 2
    blocks = cols // LANES
    frame_rows = BLOCKS * slab_rows
    rows_half = place_ref[1]

    factors = factors_on_sublanes(magnify_ref, first)
    shrinks = factors < 1.0
    lane = lax.broadcasted_iota(jnp.int32, (GROUP, LANES), 1)
    for b in range(blocks):
        column = (lane + b * LANES).astype(jnp.float32)
        at = (column + 0.5 - half) / factors + (half - 0.5)
        floor_at = jnp.floor(at)
        part = at - floor_at
        lower = max(b - 1, 0)
        upper = min(b, blocks - 2)
        if b < blocks // 2:
            base = jnp.where(shrinks, lower, upper)
        else:
            base = jnp.where(shrinks, upper, lower)
        position = floor_at.astype(jnp.int32)
        here = slice(b * LANES, (b + 1) * LANES)
        source[:, 0, here] = position - base * LANES
        low[:, 0, here] = jnp.where(
            (position >= 0) & (position < cols), rounded(1.0 - part), 0.0
        )
        high[:, 0, here] = jnp.where(
            (position >= -1) & (position < cols - 1), rounded(part), 0.0
        )

    row = lax.broadcasted_iota(jnp.int32, (frame_rows, GROUP * slab_rows), 0)
    lane_id = lax.broadcasted_iota(jnp.int32, (frame_rows, GROUP * slab_rows), 1)
    lane_factor = jnp.full((frame_rows, GROUP * slab_rows), magnify_ref[first], jnp.float32)
    for i in range(1, GROUP):
        lane_factor = jnp.where(lane_id >= i * slab_rows, magnify_ref[first + i], lane_factor)
    middle = rows_half.astype(jnp.float32)
    detector = (row + (place_ref[0] - REACH * slab_rows)).astype(jnp.float32)
    sample = (detector + 0.5 - middle) / lane_factor + (middle - 0.5)
    axial = (lane_id % slab_rows + place_ref[0]).astype(jnp.float32)
    row_table[:, pl.ds(pl.multiple_of(group * GROUP * slab_rows, LANES), GROUP * slab_rows)] = (
        jnp.maximum(0.0, 1.0 - jnp.abs(sample - axial)).astype(jnp.bfloat16)
    )

    def plane_step(i, carry):
        shrink = (magnify_ref[first + i] < 1.0).astype(jnp.int32)
        out_row = pl.multiple_of((first + i) * slab_rows, slab_rows)
        for b in range(blocks):
            here = slice(b * LANES, (b + 1) * LANES)
            if b < blocks // 2:
                base = jnp.maximum(b - shrink, 0)
            else:
                base = jnp.minimum(b - 1 + shrink, blocks - 2)
            start = pl.multiple_of(base * LANES, LANES)
            one = volume_ref[i, :, pl.ds(start, LANES)]
            two = volume_ref[i, :, pl.ds(start + LANES, LANES)]
            where_from = jnp.broadcast_to(source[i, :, here], (slab_rows, LANES))
            at_low = pick_two(one, two, where_from.astype(jnp.int16))
            at_high = pick_two(one, two, (where_from + 1).astype(jnp.int16))
            value = at_low.astype(jnp.float32) * low[i, :, here] + at_high.astype(
                jnp.float32
            ) * high[i, :, here]
            resampled[pl.ds(out_row, slab_rows), here] = value.astype(jnp.bfloat16)
        return carry

    lax.fori_loop(0, GROUP, plane_step, 0)

    @pl.when(group == pl.num_programs(0) - 1)
    def _():
        for c in range(0, cols, 512):
            frame = jnp.dot(
                row_table[...], resampled[:, c : c + 512], preferred_element_type=jnp.float32
            )
            for position, ref in enumerate((m2_ref, m1_ref, own_ref, p1_ref, p2_ref)):
                ref[:, c : c + 512] = frame[
                    position * slab_rows : (position + 1) * slab_rows
                ].astype(ref.dtype)


def backward_kernel(
    place_ref, magnify_ref, m2_ref, m1_ref, own_ref, p1_ref, p2_ref, out_ref,
    frame, row_table, smeared, source, weight0, weight1, weight2,
):
    group = pl.program_id(0)
    first = group * GROUP
    slab_rows = out_ref.shape[1]
    cols = out_ref.shape[2]
    half = cols // 2
    blocks = cols // LANES
    rows_half = place_ref[1]

    @pl.when(group == 0)
    def _():
        frame[BLOCKS * slab_rows :, :] = jnp.zeros(
            (frame.shape[0] - BLOCKS * slab_rows, frame.shape[1]), frame.dtype
        )
        for position, ref in enumerate((m2_ref, m1_ref, own_ref, p1_ref, p2_ref)):
            values = ref[...].astype(jnp.float32)
            padded = jnp.concatenate(
                [values, jnp.zeros((slab_rows, LANES), jnp.float32)], axis=1
            )
            frame[position * slab_rows : (position + 1) * slab_rows, :] = pltpu.roll(
                padded, MARGIN, 1
            ).astype(frame.dtype)

    factors = factors_on_sublanes(magnify_ref, first)
    lane = lax.broadcasted_iota(jnp.int32, (GROUP, LANES), 1)
    for b in range(blocks):
        target = (lane + b * LANES).astype(jnp.float32)
        reach = (target - (half + 0.5)) * factors + (half - 0.501)
        tap = jnp.floor(reach) + 1.0
        here = slice(b * LANES, (b + 1) * LANES)
        source[:, 0, here] = tap.astype(jnp.int32) + (MARGIN - b * LANES)
        for step, weight in enumerate((weight0, weight1, weight2)):
            at = (tap + (step + 0.5 - half)) / factors + (half - 0.5)
            weight[:, 0, here] = rounded(jnp.maximum(0.0, 1.0 - jnp.abs(at - target)))

    middle = rows_half.astype(jnp.float32)
    row = lax.broadcasted_iota(jnp.int32, (slab_rows, LANES), 0)
    lane_id = lax.broadcasted_iota(jnp.int32, (slab_rows, LANES), 1)
    axial = (row + place_ref[0]).astype(jnp.float32)
    detector = (lane_id + (place_ref[0] - REACH * slab_rows)).astype(jnp.float32)
    for i in range(GROUP):
        sample = (detector + 0.5 - middle) / magnify_ref[first + i] + (middle - 0.5)
        row_table[i * slab_rows : (i + 1) * slab_rows, :] = jnp.maximum(
            0.0, 1.0 - jnp.abs(sample - axial)
        ).astype(jnp.bfloat16)
    smeared[...] = jnp.dot(
        row_table[...], frame[...], preferred_element_type=jnp.float32
    ).astype(jnp.bfloat16)

    def plane_step(i, carry):
        in_row = pl.multiple_of(i * slab_rows, slab_rows)
        for b in range(blocks):
            here = slice(b * LANES, (b + 1) * LANES)
            one = smeared[pl.ds(in_row, slab_rows), here]
            two = smeared[pl.ds(in_row, slab_rows), (b + 1) * LANES : (b + 2) * LANES]
            where_from = jnp.broadcast_to(source[i, :, here], (slab_rows, LANES))
            value = None
            for step, weight in enumerate((weight0, weight1, weight2)):
                term = pick_two(one, two, (where_from + step).astype(jnp.int16)).astype(
                    jnp.float32
                ) * weight[i, :, here]
                value = term if value is None else value + term
            out_ref[i, :, here] = value.astype(out_ref.dtype)
        return carry

    lax.fori_loop(0, GROUP, plane_step, 0)


def whole(shape):
    return pl.BlockSpec(shape, lambda g: (0,) * len(shape))


def forward(place, magnify, volume):
    planes, slab_rows, cols = volume.shape
    band = (slab_rows, cols)
    return pl.pallas_call(
        forward_kernel,
        grid=(planes // GROUP,),
        in_specs=[
            pl.BlockSpec(memory_space=pltpu.SMEM),
            pl.BlockSpec(memory_space=pltpu.SMEM),
            pl.BlockSpec((GROUP, slab_rows, cols), lambda g: (g, 0, 0)),
        ],
        out_specs=[whole(band)] * BLOCKS,
        out_shape=[jax.ShapeDtypeStruct(band, jnp.float32)]
        + [jax.ShapeDtypeStruct(band, jnp.bfloat16)] * (BLOCKS - 1),
        scratch_shapes=[
            pltpu.VMEM((planes * slab_rows, cols), jnp.bfloat16),
            pltpu.VMEM((BLOCKS * slab_rows, planes * slab_rows), jnp.bfloat16),
            pltpu.VMEM((GROUP, 1, cols), jnp.int32),
            pltpu.VMEM((GROUP, 1, cols), jnp.float32),
            pltpu.VMEM((GROUP, 1, cols), jnp.float32),
        ],
        compiler_params=pltpu.CompilerParams(
            dimension_semantics=("arbitrary",), vmem_limit_bytes=32 << 20
        ),
        name="forward_planes",
    )(place, magnify, volume)


def backward(place, magnify, bands):
    planes = magnify.shape[0]
    slab_rows, cols = bands[0].shape
    return pl.pallas_call(
        backward_kernel,
        grid=(planes // GROUP,),
        in_specs=[
            pl.BlockSpec(memory_space=pltpu.SMEM),
            pl.BlockSpec(memory_space=pltpu.SMEM),
        ]
        + [whole((slab_rows, cols))] * BLOCKS,
        out_specs=pl.BlockSpec((GROUP, slab_rows, cols), lambda g: (g, 0, 0)),
        out_shape=jax.ShapeDtypeStruct((planes, slab_rows, cols), jnp.bfloat16),
        scratch_shapes=[
            pltpu.VMEM((LANES, cols + LANES), jnp.bfloat16),
            pltpu.VMEM((GROUP * slab_rows, LANES), jnp.bfloat16),
            pltpu.VMEM((GROUP * slab_rows, cols + LANES), jnp.bfloat16),
            pltpu.VMEM((GROUP, 1, cols), jnp.int32),
            pltpu.VMEM((GROUP, 1, cols), jnp.float32),
            pltpu.VMEM((GROUP, 1, cols), jnp.float32),
            pltpu.VMEM((GROUP, 1, cols), jnp.float32),
        ],
        compiler_params=pltpu.CompilerParams(
            dimension_semantics=("arbitrary",), vmem_limit_bytes=32 << 20
        ),
        name="backward_planes",
    )(place, magnify, *bands)


def shards(volume, magnify, goal, live_pixels):
    slab_rows, own_cols = goal.shape
    row_count = lax.axis_size("row")
    cols = own_cols * row_count
    rows_all = slab_rows * lax.axis_size("slab")
    vol_first = lax.axis_index("slab") * slab_rows
    place = jnp.stack([vol_first, jnp.int32(rows_all // 2)]).astype(jnp.int32)

    own, m2, m1, p1, p2 = forward(place, magnify, volume)
    arrived = [
        shifted(block, "slab", distance)
        for block, distance in ((m1, -1), (p1, 1), (m2, -2), (p2, 2))
    ]
    total = own
    for block in arrived:
        total = total + block.astype(jnp.float32)

    coarse = goal.astype(jnp.bfloat16)
    fine = (goal - coarse.astype(jnp.float32)).astype(jnp.bfloat16)
    coarse = jnp.where(live_pixels == 0, jnp.bfloat16(DEAD), coarse)
    message = jnp.concatenate([total.astype(jnp.bfloat16), coarse, fine], axis=1)
    gathered = lax.all_gather(message, "row", axis=0, tiled=False).astype(jnp.float32)
    projection = gathered[:, :, :cols].sum(axis=0)
    all_coarse = jnp.concatenate(
        [gathered[r, :, cols : cols + own_cols] for r in range(row_count)], axis=1
    )
    all_fine = jnp.concatenate(
        [gathered[r, :, cols + own_cols :] for r in range(row_count)], axis=1
    )
    residual = jnp.where(
        all_coarse > 0.5 * DEAD, 0.0, projection - (all_coarse + all_fine)
    ).astype(jnp.bfloat16)
    own_projection = lax.dynamic_slice_in_dim(
        projection, lax.axis_index("row") * own_cols, own_cols, axis=1
    )

    n1, q1, n2, q2 = (shifted(residual, "slab", d) for d in (-1, 1, -2, 2))
    backprojection = backward(place, magnify, (q2, q1, residual, n1, n2))
    return (own_projection, backprojection)


def solution(mesh):
    in_specs = (P("row", "slab", None), P("row"), P("slab", "row"), P("slab", "row"))
    out_specs = (P("slab", "row"), P("row", "slab", None))
    return jax.shard_map(shards, mesh=mesh, in_specs=in_specs, out_specs=out_specs, check_vma=False)
```

time: 542 us -> 89.4 us (0.16)
  the two profiles are of different devices: /device:TPU:57 before, /device:TPU:35 now
where the time goes in v1:
time: 89.4 us; the launch traced here: 89.1 us
  starting transfers between devices  37.5 us (42%)
  Pallas kernels  22.5 us (25%)
  blocking collectives  13.3 us (15%)
  waiting for transfers between devices  11.8 us (13%)
  local copies, waits for them, and re-layouts  2.91 us (3%)
    ppermute x8, starting transfers between devices, shifted(): return lax.ppermute(block, axis, route)  37.5 us
    all_gather x1, blocking collectives, shards(): lax.all_gather(message, 'row', axis=0, tiled=False).astype(jnp.float32)  13.3 us
    pallas_call x1, Pallas kernels, backward(): pl.pallas_call(backward_kernel, grid=(planes // GROUP,), in_specs=[pl.Blo...  13.3 us
    ppermute x8, waiting for transfers between devices, shifted(): return lax.ppermute(block, axis, route)  11.8 us
    pallas_call x1, Pallas kernels, forward(): pl.pallas_call(forward_kernel, grid=(planes // GROUP,), in_specs=[pl.Bloc...  9.21 us
    unnamed x10, local copies, waits for them, and re-layouts  2.26 us
  transfers between devices with their start and end apart: 8, of which 4 were waited for; matrix products, arithmetic and copies ran while one was open for 1% of the time, Pallas kernels for 0%

profile of v1, /device:TPU:35, one launch (start us, length us, event | category | flops | bytes accessed | tf_op | source)
XLA Modules:
  0.0 89.1 jit_solution(4798253424271505658)
XLA Ops:
  0.6 0.1 pad_add_fusion.place_ref
  0.7 0.0 copy-start
  0.7 1.6 %copy-done = bf16[32,16,2048]{2,1,0:T(8,128)(2,1)S(1)} copy-done((bf16[32,16,2048]{2,1,0:T(8,128)(2,1)S(1)}, bf16[32,16,2048]{2,1,0:T(8,128)(2,1)}, u32[]{:S(2)}) %copy-start) | copy-done | bytes 2097176
  2.3 0.0 copy-start.1
  2.3 0.7 copy-done.1
  3.0 0.0 copy-start.3
  3.0 0.0 copy-start.4
  3.0 9.2 %forward_planes.1 = (f32[16,2048]{1,0:T(8,128)S(1)}, bf16[16,2048]{1,0:T(8,128)(2,1)S(1)}, bf16[16,2048]{1,0:T(8,128)(2,1)S(1)}, bf16[16,2048]{1,0:T(8,128)(2,1)S(1)}, bf16[16,2048]{1,0:T(8,128)(2,1)S(1)}) custom-call(s32[2]{0:T(128)S(1)} %pad_add_fusion.place_ref, f32[32]{0:T(128)S(1)} %copy-done.1, bf16[32,16,2048]{2,1,0:T(8,128)(2,1)S(1)} %copy-done), custom_call_target="tpu_custom_call" | custom-call | tf_op jit(solution)/shard_map/forward_planes/pallas_call | solution.py:222
  12.2 7.6 %collective-permute-start = (bf16[16,2048]{1,0:T(8,128)(2,1)S(1)}, bf16[16,2048]{1,0:T(8,128)(2,1)S(1)}, u32[]{:S(2)}, u32[]{:S(2)}) collective-permute-start(bf16[16,2048]{1,0:T(8,128)(2,1)S(1)} %get-tuple-element.8), channel_id=1, source_target_pairs={{4,0},{8,4},{12,8},{16,12},{20,16},{24,20},{28,24},{32,28},{36,32}... | collective-permute-start | bytes 196616 | tf_op jit(solution)/shard_map/ppermute | solution.py:44
  19.8 0.0 copy-start.2
  19.8 1.9 %collective-permute-start.1 = (bf16[16,2048]{1,0:T(8,128)(2,1)S(1)}, bf16[16,2048]{1,0:T(8,128)(2,1)S(1)}, u32[]{:S(2)}, u32[]{:S(2)}) collective-permute-start(bf16[16,2048]{1,0:T(8,128)(2,1)S(1)} %get-tuple-element.9), channel_id=1, source_target_pairs={{0,4},{4,8},{8,12},{12,16},{16,20},{20,24},{24,28},{28,32},{32,36}... | collective-permute-start | bytes 196616 | tf_op jit(solution)/shard_map/ppermute | solution.py:44
  21.7 2.2 %collective-permute-start.2 = (bf16[16,2048]{1,0:T(8,128)(2,1)S(1)}, bf16[16,2048]{1,0:T(8,128)(2,1)S(1)}, u32[]{:S(2)}, u32[]{:S(2)}) collective-permute-start(bf16[16,2048]{1,0:T(8,128)(2,1)S(1)} %get-tuple-element.10), channel_id=1, source_target_pairs={{8,0},{12,4},{16,8},{20,12},{24,16},{28,20},{32,24},{36,28},{40,32... | collective-permute-start | bytes 196616 | tf_op jit(solution)/shard_map/ppermute | solution.py:44
  23.9 4.0 %collective-permute-start.3 = (bf16[16,2048]{1,0:T(8,128)(2,1)S(1)}, bf16[16,2048]{1,0:T(8,128)(2,1)S(1)}, u32[]{:S(2)}, u32[]{:S(2)}) collective-permute-start(bf16[16,2048]{1,0:T(8,128)(2,1)S(1)} %get-tuple-element.11), channel_id=1, source_target_pairs={{0,8},{4,12},{8,16},{12,20},{16,24},{20,28},{24,32},{28,36},{32,40... | collective-permute-start | bytes 196616 | tf_op jit(solution)/shard_map/ppermute | solution.py:44
  27.9 0.0 copy-done.3
  27.9 0.0 copy-done.4
  28.0 0.0 collective-permute-done
  28.0 0.0 collective-permute-done.1
  28.0 0.5 collective-permute-done.2
  28.5 4.2 %collective-permute-done.3 = bf16[16,2048]{1,0:T(8,128)(2,1)S(1)} collective-permute-done((bf16[16,2048]{1,0:T(8,128)(2,1)S(1)}, bf16[16,2048]{1,0:T(8,128)(2,1)S(1)}, u32[]{:S(2)}, u32[]{:S(2)}) %collective-permute-start.3) | collective-permute-done | bytes 65568 | tf_op jit(solution)/shard_map/ppermute | solution.py:44
  32.8 13.3 %all-gather = bf16[64,3072]{1,0:T(8,128)(2,1)S(1)} all-gather(bf16[16,3072]{1,0:T(8,128)(2,1)S(1)} %pad_maximum_fusion.1), channel_id=2, replica_groups=mesh['slab'=128,'row'=4] {'row'}, dimensions={0}, use_global_device_ids=true | all-gather | bytes 491520 | tf_op jit(solution)/shard_map/all_gather | solution.py:297
  46.1 0.1 bitcast_convert_fusion
  46.3 4.4 %collective-permute-start.7 = (bf16[16,2048]{1,0:T(8,128)(2,1)S(1)}, bf16[16,2048]{1,0:T(8,128)(2,1)S(1)}, u32[]{:S(2)}, u32[]{:S(2)}) collective-permute-start(bf16[16,2048]{1,0:T(8,128)(2,1)S(1)} %fusion.2.own_ref), channel_id=1, source_target_pairs={{8,0},{12,4},{16,8},{20,12},{24,16},{28,20},{32,24},{36,28},{40,32... | collective-permute-start | bytes 196616 | tf_op jit(solution)/shard_map/ppermute | solution.py:44
  50.7 13.5 %collective-permute-start.6 = (bf16[16,2048]{1,0:T(8,128)(2,1)S(1)}, bf16[16,2048]{1,0:T(8,128)(2,1)S(1)}, u32[]{:S(2)}, u32[]{:S(2)}) collective-permute-start(bf16[16,2048]{1,0:T(8,128)(2,1)S(1)} %fusion.2.own_ref), channel_id=1, source_target_pairs={{4,0},{8,4},{12,8},{16,12},{20,16},{24,20},{28,24},{32,28},{36,32}... | collective-permute-start | bytes 196616 | tf_op jit(solution)/shard_map/ppermute | solution.py:44
  64.2 1.9 %collective-permute-start.5 = (bf16[16,2048]{1,0:T(8,128)(2,1)S(1)}, bf16[16,2048]{1,0:T(8,128)(2,1)S(1)}, u32[]{:S(2)}, u32[]{:S(2)}) collective-permute-start(bf16[16,2048]{1,0:T(8,128)(2,1)S(1)} %fusion.2.own_ref), channel_id=1, source_target_pairs={{0,4},{4,8},{8,12},{12,16},{16,20},{20,24},{24,28},{28,32},{32,36}... | collective-permute-start | bytes 196616 | tf_op jit(solution)/shard_map/ppermute | solution.py:44
  66.1 1.9 %collective-permute-start.4 = (bf16[16,2048]{1,0:T(8,128)(2,1)S(1)}, bf16[16,2048]{1,0:T(8,128)(2,1)S(1)}, u32[]{:S(2)}, u32[]{:S(2)}) collective-permute-start(bf16[16,2048]{1,0:T(8,128)(2,1)S(1)} %fusion.2.own_ref), channel_id=1, source_target_pairs={{0,8},{4,12},{8,16},{12,20},{16,24},{20,28},{24,32},{28,36},{32,40... | collective-permute-start | bytes 196616 | tf_op jit(solution)/shard_map/ppermute | solution.py:44
  68.1 0.6 constant_dynamic-slice_fusion
  68.7 0.0 collective-permute-done.7.p2_ref
  68.7 0.0 collective-permute-done.6.p1_ref
  68.7 3.2 %collective-permute-done.5.m1_ref = bf16[16,2048]{1,0:T(8,128)(2,1)S(1)} collective-permute-done((bf16[16,2048]{1,0:T(8,128)(2,1)S(1)}, bf16[16,2048]{1,0:T(8,128)(2,1)S(1)}, u32[]{:S(2)}, u32[]{:S(2)}) %collective-permute-start.5) | collective-permute-done | bytes 65568 | tf_op jit(solution)/shard_map/ppermute | solution.py:44
  71.9 3.9 %collective-permute-done.4.m2_ref = bf16[16,2048]{1,0:T(8,128)(2,1)S(1)} collective-permute-done((bf16[16,2048]{1,0:T(8,128)(2,1)S(1)}, bf16[16,2048]{1,0:T(8,128)(2,1)S(1)}, u32[]{:S(2)}, u32[]{:S(2)}) %collective-permute-start.4) | collective-permute-done | bytes 65568 | tf_op jit(solution)/shard_map/ppermute | solution.py:44
  75.8 0.0 copy-done.2
  75.8 13.3 %backward_planes.1 = bf16[32,16,2048]{2,1,0:T(8,128)(2,1)} custom-call(s32[2]{0:T(128)S(1)} %pad_add_fusion.place_ref, f32[32]{0:T(128)S(1)} %copy-done.2, bf16[16,2048]{1,0:T(8,128)(2,1)S(1)} %collective-permute-done.4.m2_ref, bf16[16,2048]{1,0:T(8,128)(2,1)S(1)} %collective-permute-done.5.m1_ref, bf16[16,2048]{1,0:T(8,128)(2,1)S(1)} %fusion.2.own_ref, ...), custom_call_target="tpu_custom_call" | custom-call | tf_op jit(solution)/shard_map/backward_planes/pallas_call | solution.py:250
  (7 shorter events, 0.1 us)
Async XLA Ops:
  0.7 1.6 %copy-start = (bf16[32,16,2048]{2,1,0:T(8,128)(2,1)S(1)}, bf16[32,16,2048]{2,1,0:T(8,128)(2,1)}, u32[]{:S(2)}) copy-start(bf16[32,16,2048]{2,1,0:T(8,128)(2,1)} %volume_ref.1) | copy-start | bytes 6291460
  2.3 0.7 copy-start.1
  3.0 25.0 %copy-start.3 = (f32[16,512]{1,0:T(8,128)S(1)}, f32[16,512]{1,0:T(8,128)}, u32[]{:S(2)}) copy-start(f32[16,512]{1,0:T(8,128)} %param.6) | copy-start | bytes 98308
  3.0 25.0 %copy-start.4 = (s32[16,512]{1,0:T(8,128)S(1)}, s32[16,512]{1,0:T(8,128)}, u32[]{:S(2)}) copy-start(s32[16,512]{1,0:T(8,128)} %param.7) | copy-start | bytes 98308
  12.2 15.8 %collective-permute-start = (bf16[16,2048]{1,0:T(8,128)(2,1)S(1)}, bf16[16,2048]{1,0:T(8,128)(2,1)S(1)}, u32[]{:S(2)}, u32[]{:S(2)}) collective-permute-start(bf16[16,2048]{1,0:T(8,128)(2,1)S(1)} %get-tuple-element.8), channel_id=1, source_target_pairs={{4,0},{8,4},{12,8},{16,12},{20,16},{24,20},{28,24},{32,28},{36,32}... | collective-permute-start | bytes 196616 | tf_op jit(solution)/shard_map/ppermute | solution.py:44
  19.8 56.0 %copy-start.2 = (f32[32]{0:T(128)S(1)}, f32[32]{0:T(128)}, u32[]{:S(2)}) copy-start(f32[32]{0:T(128)} %magnify_ref.3) | copy-start | bytes 388
  19.8 8.2 %collective-permute-start.1 = (bf16[16,2048]{1,0:T(8,128)(2,1)S(1)}, bf16[16,2048]{1,0:T(8,128)(2,1)S(1)}, u32[]{:S(2)}, u32[]{:S(2)}) collective-permute-start(bf16[16,2048]{1,0:T(8,128)(2,1)S(1)} %get-tuple-element.9), channel_id=1, source_target_pairs={{0,4},{4,8},{8,12},{12,16},{16,20},{20,24},{24,28},{28,32},{32,36}... | collective-permute-start | bytes 196616 | tf_op jit(solution)/shard_map/ppermute | solution.py:44
  21.7 6.8 %collective-permute-start.2 = (bf16[16,2048]{1,0:T(8,128)(2,1)S(1)}, bf16[16,2048]{1,0:T(8,128)(2,1)S(1)}, u32[]{:S(2)}, u32[]{:S(2)}) collective-permute-start(bf16[16,2048]{1,0:T(8,128)(2,1)S(1)} %get-tuple-element.10), channel_id=1, source_target_pairs={{8,0},{12,4},{16,8},{20,12},{24,16},{28,20},{32,24},{36,28},{40,32... | collective-permute-start | bytes 196616 | tf_op jit(solution)/shard_map/ppermute | solution.py:44
  23.9 8.8 %collective-permute-start.3 = (bf16[16,2048]{1,0:T(8,128)(2,1)S(1)}, bf16[16,2048]{1,0:T(8,128)(2,1)S(1)}, u32[]{:S(2)}, u32[]{:S(2)}) collective-permute-start(bf16[16,2048]{1,0:T(8,128)(2,1)S(1)} %get-tuple-element.11), channel_id=1, source_target_pairs={{0,8},{4,12},{8,16},{12,20},{16,24},{20,28},{24,32},{28,36},{32,40... | collective-permute-start | bytes 196616 | tf_op jit(solution)/shard_map/ppermute | solution.py:44
  46.3 22.4 %collective-permute-start.7 = (bf16[16,2048]{1,0:T(8,128)(2,1)S(1)}, bf16[16,2048]{1,0:T(8,128)(2,1)S(1)}, u32[]{:S(2)}, u32[]{:S(2)}) collective-permute-start(bf16[16,2048]{1,0:T(8,128)(2,1)S(1)} %fusion.2.own_ref), channel_id=1, source_target_pairs={{8,0},{12,4},{16,8},{20,12},{24,16},{28,20},{32,24},{36,28},{40,32... | collective-permute-start | bytes 196616 | tf_op jit(solution)/shard_map/ppermute | solution.py:44
  50.7 18.0 %collective-permute-start.6 = (bf16[16,2048]{1,0:T(8,128)(2,1)S(1)}, bf16[16,2048]{1,0:T(8,128)(2,1)S(1)}, u32[]{:S(2)}, u32[]{:S(2)}) collective-permute-start(bf16[16,2048]{1,0:T(8,128)(2,1)S(1)} %fusion.2.own_ref), channel_id=1, source_target_pairs={{4,0},{8,4},{12,8},{16,12},{20,16},{24,20},{28,24},{32,28},{36,32}... | collective-permute-start | bytes 196616 | tf_op jit(solution)/shard_map/ppermute | solution.py:44
  64.2 7.7 %collective-permute-start.5 = (bf16[16,2048]{1,0:T(8,128)(2,1)S(1)}, bf16[16,2048]{1,0:T(8,128)(2,1)S(1)}, u32[]{:S(2)}, u32[]{:S(2)}) collective-permute-start(bf16[16,2048]{1,0:T(8,128)(2,1)S(1)} %fusion.2.own_ref), channel_id=1, source_target_pairs={{0,4},{4,8},{8,12},{12,16},{16,20},{20,24},{24,28},{28,32},{32,36}... | collective-permute-start | bytes 196616 | tf_op jit(solution)/shard_map/ppermute | solution.py:44
  66.1 9.7 %collective-permute-start.4 = (bf16[16,2048]{1,0:T(8,128)(2,1)S(1)}, bf16[16,2048]{1,0:T(8,128)(2,1)S(1)}, u32[]{:S(2)}, u32[]{:S(2)}) collective-permute-start(bf16[16,2048]{1,0:T(8,128)(2,1)S(1)} %fusion.2.own_ref), channel_id=1, source_target_pairs={{0,8},{4,12},{8,16},{12,20},{16,24},{20,28},{24,32},{28,36},{32,40... | collective-permute-start | bytes 196616 | tf_op jit(solution)/shard_map/ppermute | solution.py:44

commit v2 on v1

v2 whole, which is shorter than its diff:
```python
import jax
import jax.numpy as jnp
from jax import lax
from jax.experimental import pallas as pl
from jax.experimental.pallas import tpu as pltpu
from jax.sharding import PartitionSpec as P

REACH = 2
BLOCKS = 2 * REACH + 1
LANES = 128
GROUP = 8
RUN = 121
DEAD = 1e30

LANE_GATHER = lax.GatherDimensionNumbers(
    offset_dims=(),
    collapsed_slice_dims=(1,),
    start_index_map=(1,),
    operand_batching_dims=(0,),
    start_indices_batching_dims=(0,),
)


def pick(block, lanes):
    return lax.gather(
        block,
        lanes[..., None],
        LANE_GATHER,
        (1, 1),
        mode=lax.GatherScatterMode.PROMISE_IN_BOUNDS,
    )


def window(start, ref, rows, last):
    block = start // LANES
    one = ref[rows + (pl.ds(pl.multiple_of(block * LANES, LANES), LANES),)]
    following = jnp.minimum(block + 1, last)
    two = ref[rows + (pl.ds(pl.multiple_of(following * LANES, LANES), LANES),)]
    lane = lax.broadcasted_iota(jnp.int32, one.shape, 1).astype(jnp.int16)
    edge = jnp.full(one.shape, start % LANES, jnp.int32).astype(jnp.int16)
    return jnp.where(lane >= edge, one, two)


def joined(group, before, after):
    lane = lax.broadcasted_iota(jnp.int32, before.shape, 1).astype(jnp.int16)
    return jnp.where(lane < RUN - (LANES - RUN) * group, before, after)


def run_columns(group, lane):
    return lane + jnp.where(lane >= LANES - (LANES - RUN) * group, group - 1, group) * LANES


def whole_start(position, last):
    return jnp.clip(position, 0.0, last).astype(jnp.int32)


def factors_on_sublanes(magnify_ref, first):
    plane = lax.broadcasted_iota(jnp.int32, (GROUP, LANES), 0)
    factors = jnp.full((GROUP, LANES), magnify_ref[first], jnp.float32)
    for i in range(1, GROUP):
        factors = jnp.where(plane == i, magnify_ref[first + i], factors)
    return factors


def rounded(weights):
    return weights.astype(jnp.bfloat16).astype(jnp.float32)


def forward_kernel(
    magnify_ref, volume_ref, own_ref, near_ref, far_ref, send_ref,
    resampled, row_table, source, low, high,
):
    group = pl.program_id(0)
    first = group * GROUP
    slab_rows = volume_ref.shape[1]
    cols = volume_ref.shape[2]
    half = cols // 2
    blocks = cols // LANES
    frame_rows = BLOCKS * slab_rows
    vol_first = lax.axis_index("slab") * slab_rows
    middle = slab_rows * lax.axis_size("slab") // 2

    factors = factors_on_sublanes(magnify_ref, first)
    lane = lax.broadcasted_iota(jnp.int32, (GROUP, LANES), 1)
    for g in range(blocks + 1):
        column = run_columns(g, lane).astype(jnp.float32)
        at = (column + 0.5 - half) / factors + (half - 0.5)
        floor_at = jnp.floor(at)
        part = at - floor_at
        position = floor_at.astype(jnp.int32)
        here = slice(g * LANES, (g + 1) * LANES)
        source[:, here] = position & (LANES - 1)
        low[:, here] = jnp.where(
            (position >= 0) & (position < cols), rounded(1.0 - part), 0.0
        )
        high[:, here] = jnp.where(
            (position >= -1) & (position < cols - 1), rounded(part), 0.0
        )

    row = lax.broadcasted_iota(jnp.int32, (frame_rows, GROUP * slab_rows), 0)
    lane_id = lax.broadcasted_iota(jnp.int32, (frame_rows, GROUP * slab_rows), 1)
    lane_factor = jnp.full((frame_rows, GROUP * slab_rows), magnify_ref[first], jnp.float32)
    for i in range(1, GROUP):
        lane_factor = jnp.where(lane_id >= i * slab_rows, magnify_ref[first + i], lane_factor)
    detector = (row + (vol_first - REACH * slab_rows)).astype(jnp.float32)
    sample = (detector + (0.5 - middle)) / lane_factor + (middle - 0.5)
    axial = (lane_id % slab_rows + vol_first).astype(jnp.float32)
    row_table[:, pl.ds(pl.multiple_of(group * GROUP * slab_rows, LANES), GROUP * slab_rows)] = (
        jnp.maximum(0.0, 1.0 - jnp.abs(sample - axial)).astype(jnp.bfloat16)
    )

    for i in range(GROUP):
        rate = 1.0 / magnify_ref[first + i]
        out_row = pl.multiple_of((first + i) * slab_rows, slab_rows)
        before = None
        for g in range(blocks + 1):
            here = slice(g * LANES, (g + 1) * LANES)
            start = whole_start(
                (g * RUN + 0.5 - half) * rate + (half - 0.75), float(cols - LANES)
            )
            values = window(start, volume_ref, (i, slice(None)), blocks - 1)
            lanes = jnp.broadcast_to(source[i : i + 1, here], values.shape).astype(jnp.int16)
            at_low = pick(values, lanes).astype(jnp.float32)
            at_high = pick(values, (lanes + 1) & (LANES - 1)).astype(jnp.float32)
            run = (at_low * low[i : i + 1, here] + at_high * high[i : i + 1, here]).astype(
                jnp.bfloat16
            )
            if before is not None:
                resampled[pl.ds(out_row, slab_rows), (g - 1) * LANES : g * LANES] = joined(
                    g - 1, before, run
                )
            before = run

    @pl.when(group == pl.num_programs(0) - 1)
    def _():
        upward = lax.axis_index("row") % 2 == 0
        r = slab_rows
        for c in range(0, cols, 512):
            here = slice(c, c + 512)
            frame = jnp.dot(
                row_table[...], resampled[:, here], preferred_element_type=jnp.float32
            )
            own_ref[:, here] = frame[2 * r : 3 * r]
            near_ref[:, here] = jnp.where(upward, frame[3 * r : 4 * r], frame[r : 2 * r])
            far_ref[:, here] = jnp.where(upward, frame[4 * r :], frame[:r])
            send_ref[:r, here] = jnp.where(upward, frame[r : 2 * r], frame[3 * r : 4 * r]).astype(
                send_ref.dtype
            )
            send_ref[r:, here] = jnp.where(upward, frame[:r], frame[4 * r :]).astype(
                send_ref.dtype
            )


def backward_kernel(
    magnify_ref, own_ref, halo_ref, out_ref,
    frame, row_table, smeared, source, weight0, weight1, weight2,
):
    group = pl.program_id(0)
    first = group * GROUP
    slab_rows = out_ref.shape[1]
    cols = out_ref.shape[2]
    half = cols // 2
    blocks = cols // LANES
    vol_first = lax.axis_index("slab") * slab_rows
    middle = slab_rows * lax.axis_size("slab") // 2

    @pl.when(group == 0)
    def _():
        r = slab_rows
        frame[:r, :] = halo_ref[0, r:, :]
        frame[r : 2 * r, :] = halo_ref[0, :r, :]
        frame[2 * r : 3 * r, :] = own_ref[...]
        frame[3 * r : 5 * r, :] = halo_ref[1]
        frame[5 * r :, :] = jnp.zeros((frame.shape[0] - 5 * r, cols), frame.dtype)

    factors = factors_on_sublanes(magnify_ref, first)
    lane = lax.broadcasted_iota(jnp.int32, (GROUP, LANES), 1)
    for g in range(blocks + 1):
        target = run_columns(g, lane).astype(jnp.float32)
        tap = jnp.floor((target - (half + 0.5)) * factors + (half - 0.501)) + 1.0
        here = slice(g * LANES, (g + 1) * LANES)
        source[:, here] = tap.astype(jnp.int32) & (LANES - 1)
        for step, weight in enumerate((weight0, weight1, weight2)):
            column = tap + step
            at = (column + (0.5 - half)) / factors + (half - 0.5)
            weight[:, here] = jnp.where(
                (column >= 0.0) & (column < cols),
                rounded(jnp.maximum(0.0, 1.0 - jnp.abs(at - target))),
                0.0,
            )

    row = lax.broadcasted_iota(jnp.int32, (slab_rows, LANES), 0)
    lane_id = lax.broadcasted_iota(jnp.int32, (slab_rows, LANES), 1)
    axial = (row + vol_first).astype(jnp.float32)
    detector = (lane_id + (vol_first - REACH * slab_rows)).astype(jnp.float32)
    for i in range(GROUP):
        sample = (detector + (0.5 - middle)) / magnify_ref[first + i] + (middle - 0.5)
        row_table[i * slab_rows : (i + 1) * slab_rows, :] = jnp.maximum(
            0.0, 1.0 - jnp.abs(sample - axial)
        ).astype(jnp.bfloat16)
    smeared[...] = jnp.dot(
        row_table[...], frame[...], preferred_element_type=jnp.float32
    ).astype(jnp.bfloat16)

    for i in range(GROUP):
        factor = magnify_ref[first + i]
        rows = (slice(i * slab_rows, (i + 1) * slab_rows),)
        before = None
        for g in range(blocks + 1):
            here = slice(g * LANES, (g + 1) * LANES)
            start = whole_start(
                (g * RUN - (half + 0.5)) * factor + (half + 0.249), float(cols - LANES)
            )
            values = window(start, smeared, rows, blocks - 1)
            lanes = jnp.broadcast_to(source[i : i + 1, here], values.shape).astype(jnp.int16)
            total = pick(values, lanes).astype(jnp.float32) * weight0[i : i + 1, here]
            for step, weight in ((1, weight1), (2, weight2)):
                total = total + pick(values, (lanes + step) & (LANES - 1)).astype(
                    jnp.float32
                ) * weight[i : i + 1, here]
            run = total.astype(out_ref.dtype)
            if before is not None:
                out_ref[i, :, (g - 1) * LANES : g * LANES] = joined(g - 1, before, run)
            before = run


def whole(shape):
    return pl.BlockSpec(shape, lambda g: (0,) * len(shape))


PARAMS = pltpu.CompilerParams(dimension_semantics=("arbitrary",), vmem_limit_bytes=56 << 20)


def forward(magnify, volume):
    planes, slab_rows, cols = volume.shape
    band = (slab_rows, cols)
    pair = (2 * slab_rows, cols)
    run_cols = cols + LANES
    return pl.pallas_call(
        forward_kernel,
        grid=(planes // GROUP,),
        in_specs=[
            pl.BlockSpec(memory_space=pltpu.SMEM),
            pl.BlockSpec((GROUP, slab_rows, cols), lambda g: (g, 0, 0)),
        ],
        out_specs=[whole(band)] * 3 + [whole(pair)],
        out_shape=[jax.ShapeDtypeStruct(band, jnp.float32)] * 3
        + [jax.ShapeDtypeStruct(pair, jnp.bfloat16)],
        scratch_shapes=[
            pltpu.VMEM((planes * slab_rows, cols), jnp.bfloat16),
            pltpu.VMEM((BLOCKS * slab_rows, planes * slab_rows), jnp.bfloat16),
            pltpu.VMEM((GROUP, run_cols), jnp.int32),
            pltpu.VMEM((GROUP, run_cols), jnp.float32),
            pltpu.VMEM((GROUP, run_cols), jnp.float32),
        ],
        compiler_params=PARAMS,
        name="forward_planes",
    )(magnify, volume)


def backward(magnify, residual, halo):
    planes = magnify.shape[0]
    slab_rows, cols = residual.shape
    run_cols = cols + LANES
    return pl.pallas_call(
        backward_kernel,
        grid=(planes // GROUP,),
        in_specs=[
            pl.BlockSpec(memory_space=pltpu.SMEM),
            whole(residual.shape),
            whole(halo.shape),
        ],
        out_specs=pl.BlockSpec((GROUP, slab_rows, cols), lambda g: (g, 0, 0)),
        out_shape=jax.ShapeDtypeStruct((planes, slab_rows, cols), jnp.bfloat16),
        scratch_shapes=[
            pltpu.VMEM((LANES, cols), jnp.bfloat16),
            pltpu.VMEM((GROUP * slab_rows, LANES), jnp.bfloat16),
            pltpu.VMEM((GROUP * slab_rows, cols), jnp.bfloat16),
            pltpu.VMEM((GROUP, run_cols), jnp.int32),
            pltpu.VMEM((GROUP, run_cols), jnp.float32),
            pltpu.VMEM((GROUP, run_cols), jnp.float32),
            pltpu.VMEM((GROUP, run_cols), jnp.float32),
        ],
        compiler_params=PARAMS,
        name="backward_planes",
    )(magnify, residual, halo)


def both_ways(block, distance):
    slabs, members = lax.axis_size("slab"), lax.axis_size("row")
    route = []
    for s in range(slabs):
        for q in range(members):
            to = s + (distance if q % 2 == 0 else -distance)
            if 0 <= to < slabs:
                route.append((s * members + q, to * members + q))
    return lax.ppermute(block, ("slab", "row"), route)


def shards(volume, magnify, goal, live_pixels):
    slab_rows, own_cols = goal.shape
    row_count = lax.axis_size("row")
    cols = own_cols * row_count

    own, near, far, send = forward(magnify, volume)
    got = lax.ppermute(send, "row", [(q, q ^ 1) for q in range(row_count)]).astype(jnp.float32)
    near = both_ways((near + got[:slab_rows]).astype(jnp.bfloat16), 1)
    far = both_ways((far + got[slab_rows:]).astype(jnp.bfloat16), 2)
    total = own + near.astype(jnp.float32) + far.astype(jnp.float32)

    coarse = goal.astype(jnp.bfloat16)
    fine = (goal - coarse.astype(jnp.float32)).astype(jnp.bfloat16)
    coarse = jnp.where(live_pixels == 0, jnp.bfloat16(DEAD), coarse)
    message = jnp.concatenate([total.astype(jnp.bfloat16), coarse, fine], axis=1)
    gathered = lax.all_gather(message, "row", axis=0, tiled=False).astype(jnp.float32)
    projection = gathered[:, :, :cols].sum(axis=0)
    all_coarse = jnp.concatenate(
        [gathered[r, :, cols : cols + own_cols] for r in range(row_count)], axis=1
    )
    all_fine = jnp.concatenate(
        [gathered[r, :, cols + own_cols :] for r in range(row_count)], axis=1
    )
    residual = jnp.where(
        all_coarse > 0.5 * DEAD, 0.0, projection - (all_coarse + all_fine)
    ).astype(jnp.bfloat16)
    own_projection = lax.dynamic_slice_in_dim(
        projection, lax.axis_index("row") * own_cols, own_cols, axis=1
    )

    arrived = jnp.concatenate([both_ways(residual, 1), both_ways(residual, 2)], axis=0)
    halo = lax.all_gather(
        arrived, "row", axis_index_groups=[[q, q + 1] for q in range(0, row_count, 2)]
    )
    return (own_projection, backward(magnify, residual, halo))


def solution(mesh):
    in_specs = (P("row", "slab", None), P("row"), P("slab", "row"), P("slab", "row"))
    out_specs = (P("slab", "row"), P("row", "slab", None))
    return jax.shard_map(shards, mesh=mesh, in_specs=in_specs, out_specs=out_specs, check_vma=False)
```

time: 89.4 us -> 73.8 us (0.83)
  the two profiles are of different devices: /device:TPU:35 before, /device:TPU:33 now
where the time goes in v2:
time: 73.8 us; the launch traced here: 73.5 us
  blocking collectives  21.7 us (29%)
  starting transfers between devices  20.2 us (27%)
  Pallas kernels  20 us (27%)
  waiting for transfers between devices  8.11 us (11%)
  other arithmetic  2.09 us (3%)
  between operations  0.79 us (1%)
    ppermute x4, starting transfers between devices, both_ways(): return lax.ppermute(block, ('slab', 'row'), route)  17.6 us
    all_gather x1, blocking collectives, shards(): lax.all_gather(message, 'row', axis=0, tiled=False).astype(jnp.float32)  15.3 us
    pallas_call x1, Pallas kernels, backward(): pl.pallas_call(backward_kernel, grid=(planes // GROUP,), in_specs=[pl.Blo...  10.9 us
    pallas_call x1, Pallas kernels, forward(): pl.pallas_call(forward_kernel, grid=(planes // GROUP,), in_specs=[pl.Bloc...  9.05 us
    ppermute x4, waiting for transfers between devices, both_ways(): return lax.ppermute(block, ('slab', 'row'), route)  6.97 us
    all_gather x1, blocking collectives, shards(): lax.all_gather(arrived, 'row', axis_index_groups=[[q, q + 1] for q in ran...  6.36 us
    ppermute x1, starting transfers between devices, shards(): lax.ppermute(send, 'row', [(q, q ^ 1) for q in range(row_count)])  2.57 us
  transfers between devices with their start and end apart: 5, of which 3 were waited for; matrix products, arithmetic and copies ran while one was open for 1% of the time, Pallas kernels for 0%

profile of v2, /device:TPU:33, one launch (start us, length us, event | category | flops | bytes accessed | tf_op | source)
XLA Modules:
  0.0 73.5 jit_solution(15516941793791224087)
XLA Ops:
  0.6 0.0 copy-start.1
  0.6 0.0 copy-start.2
  0.6 9.0 %forward_planes.1 = (f32[16,2048]{1,0:T(8,128)}, f32[16,2048]{1,0:T(8,128)}, f32[16,2048]{1,0:T(8,128)}, bf16[32,2048]{1,0:T(8,128)(2,1)}) custom-call(f32[32]{0:T(128)} %magnify_ref.3, bf16[32,16,2048]{2,1,0:T(8,128)(2,1)} %volume_ref.1), custom_call_target="tpu_custom_call" | custom-call | tf_op jit(solution)/shard_map/forward_planes/pallas_call | solution.py:239
  9.7 2.6 %collective-permute-start = (bf16[32,2048]{1,0:T(8,128)(2,1)}, bf16[32,2048]{1,0:T(8,128)(2,1)S(1)}, u32[]{:S(2)}, u32[]{:S(2)}) collective-permute-start(bf16[32,2048]{1,0:T(8,128)(2,1)} %get-tuple-element.8), channel_id=1, source_target_pairs={{0,1},{1,0},{2,3},{3,2},{4,5},{5,4},{6,7},{7,6},{8,9},{9,8},{10,11... | collective-permute-start | bytes 393224 | tf_op jit(solution)/shard_map/ppermute | solution.py:306
  12.3 0.0 copy-done.1
  12.3 0.0 copy-done.2
  12.3 1.1 %collective-permute-done = bf16[32,2048]{1,0:T(8,128)(2,1)S(1)} collective-permute-done((bf16[32,2048]{1,0:T(8,128)(2,1)}, bf16[32,2048]{1,0:T(8,128)(2,1)S(1)}, u32[]{:S(2)}, u32[]{:S(2)}) %collective-permute-start) | collective-permute-done | bytes 131104 | tf_op jit(solution)/shard_map/ppermute | solution.py:306
  13.5 1.0 %fusion.1 = (bf16[16,2048]{1,0:T(8,128)(2,1)S(1)}, bf16[16,2048]{1,0:T(8,128)(2,1)S(1)}) fusion(f32[16,2048]{1,0:T(8,128)} %get-tuple-element.7, f32[32,2048]{1,0:T(8,128)S(1)} %convert_element_type.33, f32[16,2048]{1,0:T(8,128)} %get-tuple-element.9), kind=kLoop, calls=%fused_computation.4 | loop fusion | flops 131072 | bytes 655360 | tf_op jit(solution)/shard_map/convert_element_type | solution.py:307
  14.5 9.7 %collective-permute-start.1 = (bf16[16,2048]{1,0:T(8,128)(2,1)S(1)}, bf16[16,2048]{1,0:T(8,128)(2,1)S(1)}, u32[]{:S(2)}, u32[]{:S(2)}) collective-permute-start(bf16[16,2048]{1,0:T(8,128)(2,1)S(1)} %get-tuple-element.18), channel_id=1, source_target_pairs={{0,4},{2,6},{4,8},{5,1},{6,10},{7,3},{8,12},{9,5},{10,14},{11,7},{... | collective-permute-start | bytes 196616 | tf_op jit(solution)/shard_map/ppermute | solution.py:297
  24.2 1.9 %collective-permute-start.2 = (bf16[16,2048]{1,0:T(8,128)(2,1)S(1)}, bf16[16,2048]{1,0:T(8,128)(2,1)S(1)}, u32[]{:S(2)}, u32[]{:S(2)}) collective-permute-start(bf16[16,2048]{1,0:T(8,128)(2,1)S(1)} %get-tuple-element.19), channel_id=1, source_target_pairs={{0,8},{2,10},{4,12},{6,14},{8,16},{9,1},{10,18},{11,3},{12,20},{13... | collective-permute-start | bytes 196616 | tf_op jit(solution)/shard_map/ppermute | solution.py:297
  26.1 0.0 collective-permute-done.1
  26.1 4.0 %collective-permute-done.2 = bf16[16,2048]{1,0:T(8,128)(2,1)S(1)} collective-permute-done((bf16[16,2048]{1,0:T(8,128)(2,1)S(1)}, bf16[16,2048]{1,0:T(8,128)(2,1)S(1)}, u32[]{:S(2)}, u32[]{:S(2)}) %collective-permute-start.2) | collective-permute-done | bytes 65568 | tf_op jit(solution)/shard_map/ppermute | solution.py:297
  30.1 0.9 %add_convert_fusion = bf16[16,2048]{1,0:T(8,128)(2,1)S(1)} fusion(bf16[16,2048]{1,0:T(8,128)(2,1)S(1)} %collective-permute-done.2, f32[16,2048]{1,0:T(8,128)} %get-tuple-element.6, bf16[16,2048]{1,0:T(8,128)(2,1)S(1)} %collective-permute-done.1), kind=kLoop, calls=%fused_computation.11 | loop fusion | flops 163840 | bytes 327680 | tf_op jit(solution)/shard_map/convert_element_type | solution.py:314
  31.0 15.3 %all-gather = bf16[64,3072]{1,0:T(8,128)(2,1)S(1)} all-gather(bf16[16,3072]{1,0:T(8,128)(2,1)S(1)} %pad_maximum_fusion.2), channel_id=2, replica_groups=mesh['slab'=128,'row'=4] {'row'}, dimensions={0}, use_global_device_ids=true | all-gather | bytes 491520 | tf_op jit(solution)/shard_map/all_gather | solution.py:315
  46.4 0.1 bitcast_convert_fusion
  46.5 0.0 copy-start
  46.5 4.1 %collective-permute-start.4 = (bf16[16,2048]{1,0:T(8,128)(2,1)S(1)}, bf16[16,2048]{1,0:T(8,128)(2,1)S(1)}, u32[]{:S(2)}, u32[]{:S(2)}) collective-permute-start(bf16[16,2048]{1,0:T(8,128)(2,1)S(1)} %fusion.4.own_ref), channel_id=1, source_target_pairs={{0,8},{2,10},{4,12},{6,14},{8,16},{9,1},{10,18},{11,3},{12,20},{13... | collective-permute-start | bytes 196616 | tf_op jit(solution)/shard_map/ppermute | solution.py:297
  50.6 1.9 %collective-permute-start.3 = (bf16[16,2048]{1,0:T(8,128)(2,1)S(1)}, bf16[16,2048]{1,0:T(8,128)(2,1)S(1)}, u32[]{:S(2)}, u32[]{:S(2)}) collective-permute-start(bf16[16,2048]{1,0:T(8,128)(2,1)S(1)} %fusion.4.own_ref), channel_id=1, source_target_pairs={{0,4},{2,6},{4,8},{5,1},{6,10},{7,3},{8,12},{9,5},{10,14},{11,7},{... | collective-permute-start | bytes 196616 | tf_op jit(solution)/shard_map/ppermute | solution.py:297
  52.6 0.6 constant_dynamic-slice_fusion
  53.2 0.0 collective-permute-done.4
  53.2 3.0 %collective-permute-done.3 = bf16[16,2048]{1,0:T(8,128)(2,1)S(1)} collective-permute-done((bf16[16,2048]{1,0:T(8,128)(2,1)S(1)}, bf16[16,2048]{1,0:T(8,128)(2,1)S(1)}, u32[]{:S(2)}, u32[]{:S(2)}) %collective-permute-start.3) | collective-permute-done | bytes 65568 | tf_op jit(solution)/shard_map/ppermute | solution.py:297
  56.2 6.4 %all-gather.1 = bf16[64,2048]{1,0:T(8,128)(2,1)} all-gather(bf16[32,2048]{1,0:T(8,128)(2,1)S(1)} %pad_maximum_fusion.1), channel_id=3, replica_groups={{0,1},{2,3},{4,5},{6,7},{8,9},{10,11},{12,13},{14,15},{16,17},{18,19},{..., dimensions={0}, use_global_device_ids=true | all-gather | bytes 393216 | tf_op jit(solution)/shard_map/all_gather | solution.py:331
  62.6 0.0 copy-done
  62.6 10.9 %backward_planes.1 = bf16[32,16,2048]{2,1,0:T(8,128)(2,1)} custom-call(f32[32]{0:T(128)} %magnify_ref.3, bf16[16,2048]{1,0:T(8,128)(2,1)} %copy-done, bf16[2,32,2048]{2,1,0:T(8,128)(2,1)} %bitcast.20), custom_call_target="tpu_custom_call" | custom-call | tf_op jit(solution)/shard_map/backward_planes/pallas_call | solution.py:265
  (8 shorter events, 0.1 us)
Async XLA Ops:
  0.6 11.6 %copy-start.1 = (f32[16,512]{1,0:T(8,128)S(1)}, f32[16,512]{1,0:T(8,128)}, u32[]{:S(2)}) copy-start(f32[16,512]{1,0:T(8,128)} %param.6) | copy-start | bytes 98308
  0.6 11.6 %copy-start.2 = (s32[16,512]{1,0:T(8,128)S(1)}, s32[16,512]{1,0:T(8,128)}, u32[]{:S(2)}) copy-start(s32[16,512]{1,0:T(8,128)} %param.7) | copy-start | bytes 98308
  9.7 3.8 %collective-permute-start = (bf16[32,2048]{1,0:T(8,128)(2,1)}, bf16[32,2048]{1,0:T(8,128)(2,1)S(1)}, u32[]{:S(2)}, u32[]{:S(2)}) collective-permute-start(bf16[32,2048]{1,0:T(8,128)(2,1)} %get-tuple-element.8), channel_id=1, source_target_pairs={{0,1},{1,0},{2,3},{3,2},{4,5},{5,4},{6,7},{7,6},{8,9},{9,8},{10,11... | collective-permute-start | bytes 393224 | tf_op jit(solution)/shard_map/ppermute | solution.py:306
  14.5 11.7 %collective-permute-start.1 = (bf16[16,2048]{1,0:T(8,128)(2,1)S(1)}, bf16[16,2048]{1,0:T(8,128)(2,1)S(1)}, u32[]{:S(2)}, u32[]{:S(2)}) collective-permute-start(bf16[16,2048]{1,0:T(8,128)(2,1)S(1)} %get-tuple-element.18), channel_id=1, source_target_pairs={{0,4},{2,6},{4,8},{5,1},{6,10},{7,3},{8,12},{9,5},{10,14},{11,7},{... | collective-permute-start | bytes 196616 | tf_op jit(solution)/shard_map/ppermute | solution.py:297
  24.2 5.9 %collective-permute-start.2 = (bf16[16,2048]{1,0:T(8,128)(2,1)S(1)}, bf16[16,2048]{1,0:T(8,128)(2,1)S(1)}, u32[]{:S(2)}, u32[]{:S(2)}) collective-permute-start(bf16[16,2048]{1,0:T(8,128)(2,1)S(1)} %get-tuple-element.19), channel_id=1, source_target_pairs={{0,8},{2,10},{4,12},{6,14},{8,16},{9,1},{10,18},{11,3},{12,20},{13... | collective-permute-start | bytes 196616 | tf_op jit(solution)/shard_map/ppermute | solution.py:297
  46.5 16.1 %copy-start = (bf16[16,2048]{1,0:T(8,128)(2,1)}, bf16[16,2048]{1,0:T(8,128)(2,1)S(1)}, u32[]{:S(2)}) copy-start(bf16[16,2048]{1,0:T(8,128)(2,1)S(1)} %fusion.4.own_ref) | copy-start | bytes 196612
  46.5 6.7 %collective-permute-start.4 = (bf16[16,2048]{1,0:T(8,128)(2,1)S(1)}, bf16[16,2048]{1,0:T(8,128)(2,1)S(1)}, u32[]{:S(2)}, u32[]{:S(2)}) collective-permute-start(bf16[16,2048]{1,0:T(8,128)(2,1)S(1)} %fusion.4.own_ref), channel_id=1, source_target_pairs={{0,8},{2,10},{4,12},{6,14},{8,16},{9,1},{10,18},{11,3},{12,20},{13... | collective-permute-start | bytes 196616 | tf_op jit(solution)/shard_map/ppermute | solution.py:297
  50.6 5.6 %collective-permute-start.3 = (bf16[16,2048]{1,0:T(8,128)(2,1)S(1)}, bf16[16,2048]{1,0:T(8,128)(2,1)S(1)}, u32[]{:S(2)}, u32[]{:S(2)}) collective-permute-start(bf16[16,2048]{1,0:T(8,128)(2,1)S(1)} %fusion.4.own_ref), channel_id=1, source_target_pairs={{0,4},{2,6},{4,8},{5,1},{6,10},{7,3},{8,12},{9,5},{10,14},{11,7},{... | collective-permute-start | bytes 196616 | tf_op jit(solution)/shard_map/ppermute | solution.py:297

commit v3 on v2

v3 whole, which is shorter than its diff:
```python
import jax
import jax.numpy as jnp
from jax import lax
from jax.experimental import pallas as pl
from jax.experimental.pallas import tpu as pltpu
from jax.sharding import PartitionSpec as P

REACH = 2
BLOCKS = 2 * REACH + 1
LANES = 128
LANE_BITS = 7
FIXED_BITS = 16
FIXED = float(1 << FIXED_BITS)
GROUP = 8
SENT = 4
FETCHED = 8
CHIP_RUN = 4
RUN = 121
DEAD = 1e30

LANE_GATHER = lax.GatherDimensionNumbers(
    offset_dims=(),
    collapsed_slice_dims=(1,),
    start_index_map=(1,),
    operand_batching_dims=(0,),
    start_indices_batching_dims=(0,),
)


def pick(block, lanes):
    return lax.gather(
        block,
        lanes[..., None],
        LANE_GATHER,
        (1, 1),
        mode=lax.GatherScatterMode.PROMISE_IN_BOUNDS,
    )


def window(start, ref, rows):
    block = pl.multiple_of((start >> LANE_BITS) * LANES, LANES)
    one = ref[rows + (pl.ds(block, LANES),)]
    two = ref[rows + (pl.ds(block + LANES, LANES),)]
    lane = lax.broadcasted_iota(jnp.int32, one.shape, 1).astype(jnp.int16)
    edge = jnp.full(one.shape, start & (LANES - 1), jnp.int32).astype(jnp.int16)
    return jnp.where(lane >= edge, one, two)


def joined(group, before, after):
    lane = lax.broadcasted_iota(jnp.int32, before.shape, 1).astype(jnp.int16)
    return jnp.where(lane < RUN - (LANES - RUN) * group, before, after)


def run_columns(group, lane):
    return lane + jnp.where(lane >= LANES - (LANES - RUN) * group, group - 1, group) * LANES


def run_starts(first, stride, last):
    at = (first * FIXED).astype(jnp.int32)
    step = (stride * FIXED).astype(jnp.int32)
    while True:
        yield jnp.clip(at >> FIXED_BITS, 0, last)
        at = at + step


def factors_on_sublanes(magnify_ref, first):
    plane = lax.broadcasted_iota(jnp.int32, (GROUP, LANES), 0)
    factors = jnp.full((GROUP, LANES), magnify_ref[first], jnp.float32)
    for i in range(1, GROUP):
        factors = jnp.where(plane == i, magnify_ref[first + i], factors)
    return factors


def rounded(weights):
    return weights.astype(jnp.bfloat16).astype(jnp.float32)


def interpolated(values, lanes, weights):
    total = None
    for step, weight in enumerate(weights):
        picked = pick(values, (lanes + step) & (LANES - 1) if step else lanes)
        term = picked.astype(jnp.float32) * weight
        total = term if total is None else total + term
    return total.astype(values.dtype)


def forward_kernel(
    magnify_ref, volume_ref, own_ref, near_ref, far_ref, send_ref,
    volume, arrival, resampled, row_table, source, low, high,
):
    planes, slab_rows, cols = volume_ref.shape
    groups = planes // GROUP
    half = cols // 2
    blocks = cols // LANES
    frame_rows = BLOCKS * slab_rows
    vol_first = lax.axis_index("slab") * slab_rows
    middle = slab_rows * lax.axis_size("slab") // 2

    def fetch(part):
        planes_of = pl.ds(part * FETCHED, FETCHED)
        return pltpu.make_async_copy(
            volume_ref.at[planes_of], volume.at[planes_of, :, pl.ds(0, cols)], arrival.at[part]
        )

    for part in range(planes // FETCHED):
        fetch(part).start()

    lane = lax.broadcasted_iota(jnp.int32, (GROUP, LANES), 1)
    row = lax.broadcasted_iota(jnp.int32, (frame_rows, GROUP * slab_rows), 0)
    lane_id = lax.broadcasted_iota(jnp.int32, (frame_rows, GROUP * slab_rows), 1)
    detector = (row + (vol_first - REACH * slab_rows)).astype(jnp.float32) + (0.5 - middle)
    axial = ((lane_id & (slab_rows - 1)) + vol_first).astype(jnp.float32) - (middle - 0.5)

    def group_step(group, carry):
        first = group * GROUP
        factors = factors_on_sublanes(magnify_ref, first)
        for g in range(blocks + 1):
            column = run_columns(g, lane).astype(jnp.float32)
            at = (column + 0.5 - half) / factors + (half - 0.5)
            floor_at = jnp.floor(at)
            part = at - floor_at
            position = floor_at.astype(jnp.int32)
            here = slice(g * LANES, (g + 1) * LANES)
            source[:, here] = position & (LANES - 1)
            low[:, here] = jnp.where(
                (position >= 0) & (position < cols), rounded(1.0 - part), 0.0
            )
            high[:, here] = jnp.where(
                (position >= -1) & (position < cols - 1), rounded(part), 0.0
            )

        lane_factor = jnp.full(row.shape, magnify_ref[first], jnp.float32)
        for i in range(1, GROUP):
            lane_factor = jnp.where(lane_id >= i * slab_rows, magnify_ref[first + i], lane_factor)
        row_table[group] = jnp.maximum(
            0.0, 1.0 - jnp.abs(detector / lane_factor - axial)
        ).astype(jnp.bfloat16)

        for i in range(GROUP):
            rate = 1.0 / magnify_ref[first + i]
            starts = run_starts((0.5 - half) * rate + (half - 0.75), RUN * rate, cols - LANES)
            out_rows = slice(i * slab_rows, (i + 1) * slab_rows)
            if i % FETCHED == 0:
                fetch(group * (GROUP // FETCHED) + i // FETCHED).wait()
            before = None
            for g in range(blocks + 1):
                here = slice(g * LANES, (g + 1) * LANES)
                values = window(next(starts), volume, (first + i, slice(None)))
                lanes = jnp.broadcast_to(source[i : i + 1, here], values.shape).astype(jnp.int16)
                run = interpolated(
                    values, lanes, (low[i : i + 1, here], high[i : i + 1, here])
                )
                if before is not None:
                    resampled[group, out_rows, (g - 1) * LANES : g * LANES] = joined(
                        g - 1, before, run
                    )
                before = run
        return carry

    lax.fori_loop(0, groups, group_step, 0)

    upward = lax.axis_index("row") % 2 == 0
    r = slab_rows
    for c in range(0, cols, 512):
        here = slice(c, c + 512)
        frame = None
        for group in range(groups):
            part = jnp.dot(
                row_table[group], resampled[group, :, here], preferred_element_type=jnp.float32
            )
            frame = part if frame is None else frame + part
        own_ref[:, here] = frame[2 * r : 3 * r]
        near_ref[:, here] = jnp.where(upward, frame[3 * r : 4 * r], frame[r : 2 * r])
        far_ref[:, here] = jnp.where(upward, frame[4 * r :], frame[:r])
        send_ref[:r, here] = jnp.where(upward, frame[r : 2 * r], frame[3 * r : 4 * r]).astype(
            send_ref.dtype
        )
        send_ref[r:, here] = jnp.where(upward, frame[:r], frame[4 * r :]).astype(send_ref.dtype)


def backward_kernel(
    magnify_ref, own_ref, halo_ref, out_ref,
    out, departure, frame, row_table, smeared, source, weight0, weight1, weight2,
):
    planes, slab_rows, cols = out_ref.shape
    groups = planes // GROUP
    half = cols // 2
    blocks = cols // LANES
    vol_first = lax.axis_index("slab") * slab_rows
    middle = slab_rows * lax.axis_size("slab") // 2

    def store(part):
        planes_of = pl.ds(part * SENT, SENT)
        return pltpu.make_async_copy(out.at[planes_of], out_ref.at[planes_of], departure.at[part])

    r = slab_rows
    frame[:r, :] = halo_ref[0, r:, :]
    frame[r : 2 * r, :] = halo_ref[0, :r, :]
    frame[2 * r : 3 * r, :] = own_ref[...]
    frame[3 * r : 5 * r, :] = halo_ref[1]
    frame[5 * r :, :] = jnp.zeros((frame.shape[0] - 5 * r, cols), frame.dtype)

    row = lax.broadcasted_iota(jnp.int32, (slab_rows, LANES), 0)
    lane_id = lax.broadcasted_iota(jnp.int32, (slab_rows, LANES), 1)
    axial = (row + vol_first).astype(jnp.float32) - (middle - 0.5)
    detector = (lane_id + (vol_first - REACH * slab_rows)).astype(jnp.float32) + (0.5 - middle)
    for i in range(planes):
        row_table[i * r : (i + 1) * r, :] = jnp.maximum(
            0.0, 1.0 - jnp.abs(detector / magnify_ref[i] - axial)
        ).astype(jnp.bfloat16)
    for c in range(0, cols, 256):
        smeared[:, c : c + 256] = jnp.dot(
            row_table[...], frame[:, c : c + 256], preferred_element_type=jnp.float32
        ).astype(jnp.bfloat16)

    lane = lax.broadcasted_iota(jnp.int32, (GROUP, LANES), 1)

    def group_step(group, carry):
        first = group * GROUP
        factors = factors_on_sublanes(magnify_ref, first)
        for g in range(blocks + 1):
            target = run_columns(g, lane).astype(jnp.float32)
            tap = jnp.floor((target - (half + 0.5)) * factors + (half - 0.501)) + 1.0
            here = slice(g * LANES, (g + 1) * LANES)
            source[:, here] = tap.astype(jnp.int32) & (LANES - 1)
            for step, weight in enumerate((weight0, weight1, weight2)):
                column = tap + step
                at = (column + (0.5 - half)) / factors + (half - 0.5)
                weight[:, here] = jnp.where(
                    (column >= 0.0) & (column < cols),
                    rounded(jnp.maximum(0.0, 1.0 - jnp.abs(at - target))),
                    0.0,
                )

        for i in range(GROUP):
            factor = magnify_ref[first + i]
            starts = run_starts(
                (-half - 0.5) * factor + (half + 0.249), RUN * factor, cols - LANES
            )
            rows = (pl.ds(pl.multiple_of((first + i) * r, r), r),)
            before = None
            for g in range(blocks + 1):
                here = slice(g * LANES, (g + 1) * LANES)
                values = window(next(starts), smeared, rows)
                lanes = jnp.broadcast_to(source[i : i + 1, here], values.shape).astype(jnp.int16)
                run = interpolated(
                    values, lanes, [w[i : i + 1, here] for w in (weight0, weight1, weight2)]
                )
                if before is not None:
                    out[first + i, :, (g - 1) * LANES : g * LANES] = joined(g - 1, before, run)
                before = run
            if (i + 1) % SENT == 0:
                store(group * (GROUP // SENT) + i // SENT).start()
        return carry

    lax.fori_loop(0, groups, group_step, 0)
    for part in range(planes // SENT):
        store(part).wait()


PARAMS = pltpu.CompilerParams(vmem_limit_bytes=53 << 20)
SMEM = pl.BlockSpec(memory_space=pltpu.SMEM)
VMEM = pl.BlockSpec(memory_space=pltpu.VMEM)
ANY = pl.BlockSpec(memory_space=pl.ANY)


def forward(magnify, volume):
    planes, slab_rows, cols = volume.shape
    groups = planes // GROUP
    band = (slab_rows, cols)
    pair = (2 * slab_rows, cols)
    run_cols = cols + LANES
    return pl.pallas_call(
        forward_kernel,
        in_specs=[SMEM, ANY],
        out_specs=[VMEM] * 4,
        out_shape=[jax.ShapeDtypeStruct(band, jnp.float32)] * 3
        + [jax.ShapeDtypeStruct(pair, jnp.bfloat16)],
        scratch_shapes=[
            pltpu.VMEM((planes, slab_rows, run_cols), volume.dtype),
            pltpu.SemaphoreType.DMA((planes // FETCHED,)),
            pltpu.VMEM((groups, GROUP * slab_rows, cols), jnp.bfloat16),
            pltpu.VMEM((groups, BLOCKS * slab_rows, GROUP * slab_rows), jnp.bfloat16),
            pltpu.VMEM((GROUP, run_cols), jnp.int32),
            pltpu.VMEM((GROUP, run_cols), jnp.float32),
            pltpu.VMEM((GROUP, run_cols), jnp.float32),
        ],
        compiler_params=PARAMS,
        name="forward_planes",
    )(magnify, volume)


def backward(magnify, residual, halo):
    planes = magnify.shape[0]
    slab_rows, cols = residual.shape
    run_cols = cols + LANES
    shape = (planes, slab_rows, cols)
    return pl.pallas_call(
        backward_kernel,
        in_specs=[SMEM, VMEM, VMEM],
        out_specs=ANY,
        out_shape=jax.ShapeDtypeStruct(shape, jnp.bfloat16),
        scratch_shapes=[
            pltpu.VMEM(shape, jnp.bfloat16),
            pltpu.SemaphoreType.DMA((planes // SENT,)),
            pltpu.VMEM((LANES, cols), jnp.bfloat16),
            pltpu.VMEM((planes * slab_rows, LANES), jnp.bfloat16),
            pltpu.VMEM((planes * slab_rows, run_cols), jnp.bfloat16),
            pltpu.VMEM((GROUP, run_cols), jnp.int32),
            pltpu.VMEM((GROUP, run_cols), jnp.float32),
            pltpu.VMEM((GROUP, run_cols), jnp.float32),
            pltpu.VMEM((GROUP, run_cols), jnp.float32),
        ],
        compiler_params=PARAMS,
        name="backward_planes",
    )(magnify, residual, halo)


def both_ways(block, distance):
    slabs, members = lax.axis_size("slab"), lax.axis_size("row")
    route = []
    for s in range(slabs):
        for q in range(members):
            to = s + (distance if q % 2 == 0 else -distance)
            if 0 <= to < slabs:
                crosses = distance == 1 and s // CHIP_RUN != to // CHIP_RUN
                route.append((s * members + q, to * members + (q ^ 2 if crosses else q)))
    return lax.ppermute(block, ("slab", "row"), route)


def shards(volume, magnify, goal, live_pixels):
    slab_rows, own_cols = goal.shape
    row_count = lax.axis_size("row")
    cols = own_cols * row_count

    pairs = [[q, q + 1] for q in range(0, row_count, 2)]
    own, near, far, send = forward(magnify, volume)
    got = lax.ppermute(send, "row", [(q, q ^ 1) for q in range(row_count)]).astype(jnp.float32)
    near = both_ways((near + got[:slab_rows]).astype(jnp.bfloat16), 1)
    far = both_ways((far + got[slab_rows:]).astype(jnp.bfloat16), 2)
    total = own + near.astype(jnp.float32) + far.astype(jnp.float32)

    coarse = goal.astype(jnp.bfloat16)
    fine = (goal - coarse.astype(jnp.float32)).astype(jnp.bfloat16)
    coarse = jnp.where(live_pixels == 0, jnp.bfloat16(DEAD), coarse)
    message = jnp.concatenate([total.astype(jnp.bfloat16), coarse, fine], axis=1)
    other = lax.ppermute(message, "row", [(q, q ^ 2) for q in range(row_count)])
    total = total + other[:, :cols].astype(jnp.float32)
    message = jnp.concatenate([total.astype(jnp.bfloat16), message[:, cols:], other[:, cols:]], axis=1)
    gathered = lax.all_gather(message, "row", axis_index_groups=pairs).astype(jnp.float32)
    projection = gathered[:, :, :cols].sum(axis=0)
    lower_half = lax.axis_index("row") < 2
    mine, others = gathered[:, :, cols : cols + 2 * own_cols], gathered[:, :, cols + 2 * own_cols :]
    members = [jnp.where(lower_half, mine, others), jnp.where(lower_half, others, mine)]
    members = [half[core] for half in members for core in range(2)]
    all_coarse = jnp.concatenate([goals[:, :own_cols] for goals in members], axis=1)
    all_fine = jnp.concatenate([goals[:, own_cols:] for goals in members], axis=1)
    residual = jnp.where(
        all_coarse > 0.5 * DEAD, 0.0, projection - (all_coarse + all_fine)
    ).astype(jnp.bfloat16)
    own_projection = lax.dynamic_slice_in_dim(
        projection, lax.axis_index("row") * own_cols, own_cols, axis=1
    )

    arrived = jnp.concatenate([both_ways(residual, 1), both_ways(residual, 2)], axis=0)
    halo = lax.all_gather(arrived, "row", axis_index_groups=pairs)
    return (own_projection, backward(magnify, residual, halo))


def solution(mesh):
    in_specs = (P("row", "slab", None), P("row"), P("slab", "row"), P("slab", "row"))
    out_specs = (P("slab", "row"), P("row", "slab", None))
    return jax.shard_map(shards, mesh=mesh, in_specs=in_specs, out_specs=out_specs, check_vma=False)
```

time: 73.8 us -> 67.9 us (0.920)
  blocking collectives: 21.7 us -> 8.96 us
  waiting for transfers between devices: 8.11 us -> 16.1 us
  Pallas kernels: 20 us -> 13.4 us
  starting transfers between devices: 20.2 us -> 26.7 us
  other arithmetic: 2.09 us -> 0.25 us
    all_gather x2, blocking collectives: 21.7 us -> 8.96 us  [the longest x1 6.93 us: shards(): halo = lax.all_gather(arrived, 'row', axis_index_groups=pairs)]
    ppermute x0 -> x1, waiting for transfers between devices: none -> 9.53 us  [shards(): other = lax.ppermute(message, 'row', [(q, q ^ 2) for q in range(row_count)])]
    pallas_call x2, Pallas kernels: 20 us -> 13.4 us  [the longest x1 7.06 us: backward(): pl.pallas_call(backward_kernel, in_specs=[SMEM, VMEM, VMEM], out_specs=AN...]
    ppermute x4, starting transfers between devices: 17.6 us -> 22.1 us  [both_ways(): return lax.ppermute(block, ('slab', 'row'), route)]
    ppermute x0 -> x1, starting transfers between devices: none -> 1.97 us  [shards(): other = lax.ppermute(message, 'row', [(q, q ^ 2) for q in range(row_count)])]
    ppermute x4, waiting for transfers between devices: 6.97 us -> 5.67 us  [both_ways(): return lax.ppermute(block, ('slab', 'row'), route)]
    convert_element_type x1, other arithmetic: 1.01 us -> 0.03 us  [shards(): near = both_ways((near + got[:slab_rows]).astype(jnp.bfloat16), 1)]
    convert_element_type x1 -> x2, other arithmetic: 0.93 us -> 0.06 us  [shards(): total.astype(jnp.bfloat16)]
  transfers between devices with their start and end apart: 5 -> 6, of which waited for: 3 -> 4; matrix products, arithmetic and copies ran while one was open for 1% -> 1% of each run, Pallas kernels for 0% -> 0%
where the time goes in v3:
time: 67.9 us; the launch traced here: 67.6 us
  starting transfers between devices  26.7 us (39%)
  waiting for transfers between devices  16.1 us (24%)
  Pallas kernels  13.4 us (20%)
  blocking collectives  8.96 us (13%)
  local copies, waits for them, and re-layouts  1.34 us (2%)
  between operations  0.86 us (1%)
    ppermute x4, starting transfers between devices, both_ways(): return lax.ppermute(block, ('slab', 'row'), route)  22.1 us
    ppermute x1, waiting for transfers between devices, shards(): other = lax.ppermute(message, 'row', [(q, q ^ 2) for q in range(row_count)])  9.53 us
    pallas_call x1, Pallas kernels, backward(): pl.pallas_call(backward_kernel, in_specs=[SMEM, VMEM, VMEM], out_specs=AN...  7.06 us
    all_gather x1, blocking collectives, shards(): halo = lax.all_gather(arrived, 'row', axis_index_groups=pairs)  6.93 us
    pallas_call x1, Pallas kernels, forward(): pl.pallas_call(forward_kernel, in_specs=[SMEM, ANY], out_specs=[VMEM] * 4...  6.35 us
    ppermute x4, waiting for transfers between devices, both_ways(): return lax.ppermute(block, ('slab', 'row'), route)  5.67 us
    ppermute x1, starting transfers between devices, shards(): lax.ppermute(send, 'row', [(q, q ^ 1) for q in range(row_count)])  2.58 us
    all_gather x1, blocking collectives, shards(): lax.all_gather(message, 'row', axis_index_groups=pairs).astype(jnp.float32)  2.03 us
  transfers between devices with their start and end apart: 6, of which 4 were waited for; matrix products, arithmetic and copies ran while one was open for 1% of the time, Pallas kernels for 0%

profile of v3, /device:TPU:33, one launch (start us, length us, event | category | flops | bytes accessed | tf_op | source)
XLA Modules:
  0.0 67.6 jit_solution(6230575352994649532)
XLA Ops:
  0.6 0.0 copy-start
  0.6 0.6 copy-done
  1.3 0.0 copy-start.2
  1.3 0.0 copy-start.3
  1.3 6.4 %forward_planes.1 = (f32[16,2048]{1,0:T(8,128)S(1)}, f32[16,2048]{1,0:T(8,128)S(1)}, f32[16,2048]{1,0:T(8,128)S(1)}, bf16[32,2048]{1,0:T(8,128)(2,1)S(1)}) custom-call(f32[32]{0:T(128)S(1)} %copy-done, bf16[32,16,2048]{2,1,0:T(8,128)(2,1)} %volume_ref.1), custom_call_target="tpu_custom_call" | custom-call | tf_op jit(solution)/shard_map/forward_planes/pallas_call | solution.py:273
  7.7 2.6 %collective-permute-start = (bf16[32,2048]{1,0:T(8,128)(2,1)S(1)}, bf16[32,2048]{1,0:T(8,128)(2,1)S(1)}, u32[]{:S(2)}, u32[]{:S(2)}) collective-permute-start(bf16[32,2048]{1,0:T(8,128)(2,1)S(1)} %get-tuple-element.8), channel_id=1, source_target_pairs={{0,1},{1,0},{2,3},{3,2},{4,5},{5,4},{6,7},{7,6},{8,9},{9,8},{10,11... | collective-permute-start | bytes 393224 | tf_op jit(solution)/shard_map/ppermute | solution.py:338
  10.2 0.0 copy-done.2
  10.3 0.0 copy-done.3
  10.3 0.9 %collective-permute-done = bf16[32,2048]{1,0:T(8,128)(2,1)S(1)} collective-permute-done((bf16[32,2048]{1,0:T(8,128)(2,1)S(1)}, bf16[32,2048]{1,0:T(8,128)(2,1)S(1)}, u32[]{:S(2)}, u32[]{:S(2)}) %collective-permute-start) | collective-permute-done | bytes 131104 | tf_op jit(solution)/shard_map/ppermute | solution.py:338
  11.3 12.7 %collective-permute-start.1 = (bf16[16,2048]{1,0:T(8,128)(2,1)S(1)}, bf16[16,2048]{1,0:T(8,128)(2,1)S(1)}, u32[]{:S(2)}, u32[]{:S(2)}) collective-permute-start(bf16[16,2048]{1,0:T(8,128)(2,1)S(1)} %get-tuple-element.12), channel_id=1, source_target_pairs={{0,4},{2,6},{4,8},{5,1},{6,10},{7,3},{8,12},{9,5},{10,14},{11,7},{... | collective-permute-start | bytes 196616 | tf_op jit(solution)/shard_map/ppermute | solution.py:328
  24.0 1.9 %collective-permute-start.2 = (bf16[16,2048]{1,0:T(8,128)(2,1)S(1)}, bf16[16,2048]{1,0:T(8,128)(2,1)S(1)}, u32[]{:S(2)}, u32[]{:S(2)}) collective-permute-start(bf16[16,2048]{1,0:T(8,128)(2,1)S(1)} %get-tuple-element.13), channel_id=1, source_target_pairs={{0,8},{2,10},{4,12},{6,14},{8,16},{9,1},{10,18},{11,3},{12,20},{13... | collective-permute-start | bytes 196616 | tf_op jit(solution)/shard_map/ppermute | solution.py:328
  26.0 0.0 collective-permute-done.1
  26.0 4.0 %collective-permute-done.2 = bf16[16,2048]{1,0:T(8,128)(2,1)S(1)} collective-permute-done((bf16[16,2048]{1,0:T(8,128)(2,1)S(1)}, bf16[16,2048]{1,0:T(8,128)(2,1)S(1)}, u32[]{:S(2)}, u32[]{:S(2)}) %collective-permute-start.2) | collective-permute-done | bytes 65568 | tf_op jit(solution)/shard_map/ppermute | solution.py:328
  30.0 2.0 %collective-permute-start.3 = (bf16[16,3072]{1,0:T(8,128)(2,1)S(1)}, bf16[16,3072]{1,0:T(8,128)(2,1)S(1)}, u32[]{:S(2)}, u32[]{:S(2)}) collective-permute-start(bf16[16,3072]{1,0:T(8,128)(2,1)S(1)} %pad_maximum_fusion.3), channel_id=1, source_target_pairs={{0,2},{1,3},{2,0},{3,1},{4,6},{5,7},{6,4},{7,5},{8,10},{9,11},{10,... | collective-permute-start | bytes 294920 | tf_op jit(solution)/shard_map/ppermute | solution.py:347
  32.0 9.5 %collective-permute-done.3 = bf16[16,3072]{1,0:T(8,128)(2,1)S(1)} collective-permute-done((bf16[16,3072]{1,0:T(8,128)(2,1)S(1)}, bf16[16,3072]{1,0:T(8,128)(2,1)S(1)}, u32[]{:S(2)}, u32[]{:S(2)}) %collective-permute-start.3) | collective-permute-done | bytes 98336 | tf_op jit(solution)/shard_map/ppermute | solution.py:347
  41.6 0.0 copy-start.1
  41.6 2.0 %all-gather = bf16[32,4096]{1,0:T(8,128)(2,1)S(1)} all-gather(bf16[16,4096]{1,0:T(8,128)(2,1)S(1)} %pad_maximum_fusion), channel_id=2, replica_groups={{0,1},{2,3},{4,5},{6,7},{8,9},{10,11},{12,13},{14,15},{16,17},{18,19},{..., dimensions={0}, use_global_device_ids=true | all-gather | bytes 393216 | tf_op jit(solution)/shard_map/all_gather | solution.py:350
  43.8 3.9 %collective-permute-start.5 = (bf16[16,2048]{1,0:T(8,128)(2,1)S(1)}, bf16[16,2048]{1,0:T(8,128)(2,1)S(1)}, u32[]{:S(2)}, u32[]{:S(2)}) collective-permute-start(bf16[16,2048]{1,0:T(8,128)(2,1)S(1)} %fusion.4.own_ref), channel_id=1, source_target_pairs={{0,8},{2,10},{4,12},{6,14},{8,16},{9,1},{10,18},{11,3},{12,20},{13... | collective-permute-start | bytes 196616 | tf_op jit(solution)/shard_map/ppermute | solution.py:328
  47.7 3.6 %collective-permute-start.4 = (bf16[16,2048]{1,0:T(8,128)(2,1)S(1)}, bf16[16,2048]{1,0:T(8,128)(2,1)S(1)}, u32[]{:S(2)}, u32[]{:S(2)}) collective-permute-start(bf16[16,2048]{1,0:T(8,128)(2,1)S(1)} %fusion.4.own_ref), channel_id=1, source_target_pairs={{0,4},{2,6},{4,8},{5,1},{6,10},{7,3},{8,12},{9,5},{10,14},{11,7},{... | collective-permute-start | bytes 196616 | tf_op jit(solution)/shard_map/ppermute | solution.py:328
  51.3 0.6 constant_dynamic-slice_fusion
  51.9 0.0 collective-permute-done.5
  51.9 1.7 %collective-permute-done.4 = bf16[16,2048]{1,0:T(8,128)(2,1)S(1)} collective-permute-done((bf16[16,2048]{1,0:T(8,128)(2,1)S(1)}, bf16[16,2048]{1,0:T(8,128)(2,1)S(1)}, u32[]{:S(2)}, u32[]{:S(2)}) %collective-permute-start.4) | collective-permute-done | bytes 65568 | tf_op jit(solution)/shard_map/ppermute | solution.py:328
  53.6 6.9 %all-gather.1 = bf16[64,2048]{1,0:T(8,128)(2,1)S(1)} all-gather(bf16[32,2048]{1,0:T(8,128)(2,1)S(1)} %pad_maximum_fusion.2), channel_id=3, replica_groups={{0,1},{2,3},{4,5},{6,7},{8,9},{10,11},{12,13},{14,15},{16,17},{18,19},{..., dimensions={0}, use_global_device_ids=true | all-gather | bytes 393216 | tf_op jit(solution)/shard_map/all_gather | solution.py:366
  60.6 0.0 copy-done.1
  60.6 7.1 %backward_planes.1 = bf16[32,16,2048]{2,1,0:T(8,128)(2,1)} custom-call(f32[32]{0:T(128)S(1)} %copy-done.1, bf16[16,2048]{1,0:T(8,128)(2,1)S(1)} %fusion.4.own_ref, bf16[2,32,2048]{2,1,0:T(8,128)(2,1)S(1)} %bitcast.12), custom_call_target="tpu_custom_call" | custom-call | tf_op jit(solution)/shard_map/backward_planes/pallas_call | solution.py:298
  (19 shorter events, 0.3 us)
Async XLA Ops:
  0.6 0.7 copy-start
  1.3 9.0 %copy-start.2 = (f32[16,512]{1,0:T(8,128)S(1)}, f32[16,512]{1,0:T(8,128)}, u32[]{:S(2)}) copy-start(f32[16,512]{1,0:T(8,128)} %param.6) | copy-start | bytes 98308
  1.3 9.0 %copy-start.3 = (s32[16,512]{1,0:T(8,128)S(1)}, s32[16,512]{1,0:T(8,128)}, u32[]{:S(2)}) copy-start(s32[16,512]{1,0:T(8,128)} %param.7) | copy-start | bytes 98308
  7.7 3.6 %collective-permute-start = (bf16[32,2048]{1,0:T(8,128)(2,1)S(1)}, bf16[32,2048]{1,0:T(8,128)(2,1)S(1)}, u32[]{:S(2)}, u32[]{:S(2)}) collective-permute-start(bf16[32,2048]{1,0:T(8,128)(2,1)S(1)} %get-tuple-element.8), channel_id=1, source_target_pairs={{0,1},{1,0},{2,3},{3,2},{4,5},{5,4},{6,7},{7,6},{8,9},{9,8},{10,11... | collective-permute-start | bytes 393224 | tf_op jit(solution)/shard_map/ppermute | solution.py:338
  11.3 14.7 %collective-permute-start.1 = (bf16[16,2048]{1,0:T(8,128)(2,1)S(1)}, bf16[16,2048]{1,0:T(8,128)(2,1)S(1)}, u32[]{:S(2)}, u32[]{:S(2)}) collective-permute-start(bf16[16,2048]{1,0:T(8,128)(2,1)S(1)} %get-tuple-element.12), channel_id=1, source_target_pairs={{0,4},{2,6},{4,8},{5,1},{6,10},{7,3},{8,12},{9,5},{10,14},{11,7},{... | collective-permute-start | bytes 196616 | tf_op jit(solution)/shard_map/ppermute | solution.py:328
  24.0 5.9 %collective-permute-start.2 = (bf16[16,2048]{1,0:T(8,128)(2,1)S(1)}, bf16[16,2048]{1,0:T(8,128)(2,1)S(1)}, u32[]{:S(2)}, u32[]{:S(2)}) collective-permute-start(bf16[16,2048]{1,0:T(8,128)(2,1)S(1)} %get-tuple-element.13), channel_id=1, source_target_pairs={{0,8},{2,10},{4,12},{6,14},{8,16},{9,1},{10,18},{11,3},{12,20},{13... | collective-permute-start | bytes 196616 | tf_op jit(solution)/shard_map/ppermute | solution.py:328
  30.0 11.5 %collective-permute-start.3 = (bf16[16,3072]{1,0:T(8,128)(2,1)S(1)}, bf16[16,3072]{1,0:T(8,128)(2,1)S(1)}, u32[]{:S(2)}, u32[]{:S(2)}) collective-permute-start(bf16[16,3072]{1,0:T(8,128)(2,1)S(1)} %pad_maximum_fusion.3), channel_id=1, source_target_pairs={{0,2},{1,3},{2,0},{3,1},{4,6},{5,7},{6,4},{7,5},{8,10},{9,11},{10,... | collective-permute-start | bytes 294920 | tf_op jit(solution)/shard_map/ppermute | solution.py:347
  41.6 19.0 %copy-start.1 = (f32[32]{0:T(128)S(1)}, f32[32]{0:T(128)}, u32[]{:S(2)}) copy-start(f32[32]{0:T(128)} %magnify_ref.3) | copy-start | bytes 388
  43.8 8.1 %collective-permute-start.5 = (bf16[16,2048]{1,0:T(8,128)(2,1)S(1)}, bf16[16,2048]{1,0:T(8,128)(2,1)S(1)}, u32[]{:S(2)}, u32[]{:S(2)}) collective-permute-start(bf16[16,2048]{1,0:T(8,128)(2,1)S(1)} %fusion.4.own_ref), channel_id=1, source_target_pairs={{0,8},{2,10},{4,12},{6,14},{8,16},{9,1},{10,18},{11,3},{12,20},{13... | collective-permute-start | bytes 196616 | tf_op jit(solution)/shard_map/ppermute | solution.py:328
  47.7 5.9 %collective-permute-start.4 = (bf16[16,2048]{1,0:T(8,128)(2,1)S(1)}, bf16[16,2048]{1,0:T(8,128)(2,1)S(1)}, u32[]{:S(2)}, u32[]{:S(2)}) collective-permute-start(bf16[16,2048]{1,0:T(8,128)(2,1)S(1)} %fusion.4.own_ref), channel_id=1, source_target_pairs={{0,4},{2,6},{4,8},{5,1},{6,10},{7,3},{8,12},{9,5},{10,14},{11,7},{... | collective-permute-start | bytes 196616 | tf_op jit(solution)/shard_map/ppermute | solution.py:328

commit v4 on v3

--- a/solution.py
+++ b/solution.py
@@ -14,7 +14,6 @@
 GROUP = 8
 SENT = 4
 FETCHED = 8
-CHIP_RUN = 4
 RUN = 121
 DEAD = 1e30
 
@@ -316,15 +315,29 @@
     )(magnify, residual, halo)
 
 
-def both_ways(block, distance):
+def reaches(slab, other, slab_rows, rows_all):
+    half = rows_all / 2
+    spread = (REACH * slab_rows - 3.0) / (half + 1.0)
+    least, most = slab * slab_rows - 1.1, (slab + 1) * slab_rows + 0.1
+    for detector in range(other * slab_rows, (other + 1) * slab_rows):
+        from_middle = detector + 0.5 - half
+        ends = (from_middle / (1.0 - spread), from_middle / (1.0 + spread))
+        if max(ends) + half - 0.5 > least and min(ends) + half - 0.5 < most:
+            return True
+    return False
+
+
+def both_ways(block, distance, samples):
+    slab_rows = block.shape[0]
     slabs, members = lax.axis_size("slab"), lax.axis_size("row")
     route = []
     for s in range(slabs):
         for q in range(members):
             to = s + (distance if q % 2 == 0 else -distance)
             if 0 <= to < slabs:
-                crosses = distance == 1 and s // CHIP_RUN != to // CHIP_RUN
-                route.append((s * members + q, to * members + (q ^ 2 if crosses else q)))
+                rows_of, block_of = (s, to) if samples else (to, s)
+                if reaches(rows_of, block_of, slab_rows, slab_rows * slabs):
+                    route.append((s * members + q, to * members + q))
     return lax.ppermute(block, ("slab", "row"), route)
 
 
@@ -336,8 +349,8 @@
     pairs = [[q, q + 1] for q in range(0, row_count, 2)]
     own, near, far, send = forward(magnify, volume)
     got = lax.ppermute(send, "row", [(q, q ^ 1) for q in range(row_count)]).astype(jnp.float32)
-    near = both_ways((near + got[:slab_rows]).astype(jnp.bfloat16), 1)
-    far = both_ways((far + got[slab_rows:]).astype(jnp.bfloat16), 2)
+    near = both_ways((near + got[:slab_rows]).astype(jnp.bfloat16), 1, True)
+    far = both_ways((far + got[slab_rows:]).astype(jnp.bfloat16), 2, True)
     total = own + near.astype(jnp.float32) + far.astype(jnp.float32)
 
     coarse = goal.astype(jnp.bfloat16)
@@ -362,7 +375,7 @@
         projection, lax.axis_index("row") * own_cols, own_cols, axis=1
     )
 
-    arrived = jnp.concatenate([both_ways(residual, 1), both_ways(residual, 2)], axis=0)
+    arrived = jnp.concatenate([both_ways(residual, 1, False), both_ways(residual, 2, False)], axis=0)
     halo = lax.all_gather(arrived, "row", axis_index_groups=pairs)
     return (own_projection, backward(magnify, residual, halo))
 

time: 67.9 us -> 63.7 us (0.938)
  the two profiles are of different devices: /device:TPU:33 before, /device:TPU:57 now
where the time goes in v4:
time: 63.7 us; the launch traced here: 63.4 us
  starting transfers between devices  31.9 us (50%)
  Pallas kernels  13.4 us (21%)
  waiting for transfers between devices  10.5 us (16%)
  blocking collectives  5.09 us (8%)
  local copies, waits for them, and re-layouts  1.34 us (2%)
  between operations  0.86 us (1%)
    ppermute x4, starting transfers between devices, both_ways(): return lax.ppermute(block, ('slab', 'row'), route)  21.4 us
    ppermute x1, starting transfers between devices, shards(): other = lax.ppermute(message, 'row', [(q, q ^ 2) for q in range(row_count)])  7.94 us
    pallas_call x1, Pallas kernels, backward(): pl.pallas_call(backward_kernel, in_specs=[SMEM, VMEM, VMEM], out_specs=AN...  7.06 us
    ppermute x4, waiting for transfers between devices, both_ways(): return lax.ppermute(block, ('slab', 'row'), route)  6.52 us
    pallas_call x1, Pallas kernels, forward(): pl.pallas_call(forward_kernel, in_specs=[SMEM, ANY], out_specs=[VMEM] * 4...  6.35 us
    ppermute x1, waiting for transfers between devices, shards(): other = lax.ppermute(message, 'row', [(q, q ^ 2) for q in range(row_count)])  3.1 us
    all_gather x1, blocking collectives, shards(): halo = lax.all_gather(arrived, 'row', axis_index_groups=pairs)  2.83 us
    ppermute x1, starting transfers between devices, shards(): lax.ppermute(send, 'row', [(q, q ^ 1) for q in range(row_count)])  2.58 us
  transfers between devices with their start and end apart: 6, of which 4 were waited for; matrix products, arithmetic and copies ran while one was open for 1% of the time, Pallas kernels for 0%

profile of v4, /device:TPU:57, one launch (start us, length us, event | category | flops | bytes accessed | tf_op | source)
XLA Modules:
  0.0 63.4 jit_solution(8333849432054138474)
XLA Ops:
  0.6 0.0 copy-start
  0.6 0.6 %copy-done = f32[32]{0:T(128)S(1)} copy-done((f32[32]{0:T(128)S(1)}, f32[32]{0:T(128)}, u32[]{:S(2)}) %copy-start) | copy-done | bytes 152
  1.3 0.0 copy-start.2
  1.3 0.0 copy-start.3
  1.3 6.4 %forward_planes.1 = (f32[16,2048]{1,0:T(8,128)S(1)}, f32[16,2048]{1,0:T(8,128)S(1)}, f32[16,2048]{1,0:T(8,128)S(1)}, bf16[32,2048]{1,0:T(8,128)(2,1)S(1)}) custom-call(f32[32]{0:T(128)S(1)} %copy-done, bf16[32,16,2048]{2,1,0:T(8,128)(2,1)} %volume_ref.1), custom_call_target="tpu_custom_call" | custom-call | tf_op jit(solution)/shard_map/forward_planes/pallas_call | solution.py:272
  7.7 2.6 %collective-permute-start = (bf16[32,2048]{1,0:T(8,128)(2,1)S(1)}, bf16[32,2048]{1,0:T(8,128)(2,1)S(1)}, u32[]{:S(2)}, u32[]{:S(2)}) collective-permute-start(bf16[32,2048]{1,0:T(8,128)(2,1)S(1)} %get-tuple-element.8), channel_id=1, source_target_pairs={{0,1},{1,0},{2,3},{3,2},{4,5},{5,4},{6,7},{7,6},{8,9},{9,8},{10,11... | collective-permute-start | bytes 393224 | tf_op jit(solution)/shard_map/ppermute | solution.py:351
  10.2 0.0 copy-done.2
  10.3 0.0 copy-done.3
  10.3 0.9 %collective-permute-done = bf16[32,2048]{1,0:T(8,128)(2,1)S(1)} collective-permute-done((bf16[32,2048]{1,0:T(8,128)(2,1)S(1)}, bf16[32,2048]{1,0:T(8,128)(2,1)S(1)}, u32[]{:S(2)}, u32[]{:S(2)}) %collective-permute-start) | collective-permute-done | bytes 131104 | tf_op jit(solution)/shard_map/ppermute | solution.py:351
  11.3 10.6 %collective-permute-start.1 = (bf16[16,2048]{1,0:T(8,128)(2,1)S(1)}, bf16[16,2048]{1,0:T(8,128)(2,1)S(1)}, u32[]{:S(2)}, u32[]{:S(2)}) collective-permute-start(bf16[16,2048]{1,0:T(8,128)(2,1)S(1)} %get-tuple-element.12), channel_id=1, source_target_pairs={{0,4},{2,6},{4,8},{5,1},{6,10},{7,3},{8,12},{9,5},{10,14},{11,7},{... | collective-permute-start | bytes 196616 | tf_op jit(solution)/shard_map/ppermute | solution.py:341
  21.9 1.9 %collective-permute-start.2 = (bf16[16,2048]{1,0:T(8,128)(2,1)S(1)}, bf16[16,2048]{1,0:T(8,128)(2,1)S(1)}, u32[]{:S(2)}, u32[]{:S(2)}) collective-permute-start(bf16[16,2048]{1,0:T(8,128)(2,1)S(1)} %get-tuple-element.13), channel_id=1, source_target_pairs={{0,8},{2,10},{4,12},{6,14},{8,16},{9,1},{10,18},{11,3},{12,20},{13... | collective-permute-start | bytes 196616 | tf_op jit(solution)/shard_map/ppermute | solution.py:341
  23.8 0.0 collective-permute-done.1
  23.8 4.0 %collective-permute-done.2 = bf16[16,2048]{1,0:T(8,128)(2,1)S(1)} collective-permute-done((bf16[16,2048]{1,0:T(8,128)(2,1)S(1)}, bf16[16,2048]{1,0:T(8,128)(2,1)S(1)}, u32[]{:S(2)}, u32[]{:S(2)}) %collective-permute-start.2) | collective-permute-done | bytes 65568 | tf_op jit(solution)/shard_map/ppermute | solution.py:341
  27.8 7.9 %collective-permute-start.3 = (bf16[16,3072]{1,0:T(8,128)(2,1)S(1)}, bf16[16,3072]{1,0:T(8,128)(2,1)S(1)}, u32[]{:S(2)}, u32[]{:S(2)}) collective-permute-start(bf16[16,3072]{1,0:T(8,128)(2,1)S(1)} %pad_maximum_fusion.3), channel_id=1, source_target_pairs={{0,2},{1,3},{2,0},{3,1},{4,6},{5,7},{6,4},{7,5},{8,10},{9,11},{10,... | collective-permute-start | bytes 294920 | tf_op jit(solution)/shard_map/ppermute | solution.py:360
  35.8 3.1 %collective-permute-done.3 = bf16[16,3072]{1,0:T(8,128)(2,1)S(1)} collective-permute-done((bf16[16,3072]{1,0:T(8,128)(2,1)S(1)}, bf16[16,3072]{1,0:T(8,128)(2,1)S(1)}, u32[]{:S(2)}, u32[]{:S(2)}) %collective-permute-start.3) | collective-permute-done | bytes 98336 | tf_op jit(solution)/shard_map/ppermute | solution.py:360
  38.9 0.0 copy-start.1
  39.0 2.3 %all-gather = bf16[32,4096]{1,0:T(8,128)(2,1)S(1)} all-gather(bf16[16,4096]{1,0:T(8,128)(2,1)S(1)} %pad_maximum_fusion), channel_id=2, replica_groups={{0,1},{2,3},{4,5},{6,7},{8,9},{10,11},{12,13},{14,15},{16,17},{18,19},{..., dimensions={0}, use_global_device_ids=true | all-gather | bytes 393216 | tf_op jit(solution)/shard_map/all_gather | solution.py:363
  41.4 6.0 %collective-permute-start.5 = (bf16[16,2048]{1,0:T(8,128)(2,1)S(1)}, bf16[16,2048]{1,0:T(8,128)(2,1)S(1)}, u32[]{:S(2)}, u32[]{:S(2)}) collective-permute-start(bf16[16,2048]{1,0:T(8,128)(2,1)S(1)} %fusion.4.own_ref), channel_id=1, source_target_pairs={{0,8},{2,10},{4,12},{6,14},{8,16},{9,1},{10,18},{11,3},{12,20},{13... | collective-permute-start | bytes 196616 | tf_op jit(solution)/shard_map/ppermute | solution.py:341
  47.5 2.8 %collective-permute-start.4 = (bf16[16,2048]{1,0:T(8,128)(2,1)S(1)}, bf16[16,2048]{1,0:T(8,128)(2,1)S(1)}, u32[]{:S(2)}, u32[]{:S(2)}) collective-permute-start(bf16[16,2048]{1,0:T(8,128)(2,1)S(1)} %fusion.4.own_ref), channel_id=1, source_target_pairs={{0,4},{2,6},{4,8},{5,1},{6,10},{7,3},{8,12},{9,5},{10,14},{11,7},{... | collective-permute-start | bytes 196616 | tf_op jit(solution)/shard_map/ppermute | solution.py:341
  50.3 0.6 constant_dynamic-slice_fusion
  50.9 0.0 collective-permute-done.5
  50.9 2.6 %collective-permute-done.4 = bf16[16,2048]{1,0:T(8,128)(2,1)S(1)} collective-permute-done((bf16[16,2048]{1,0:T(8,128)(2,1)S(1)}, bf16[16,2048]{1,0:T(8,128)(2,1)S(1)}, u32[]{:S(2)}, u32[]{:S(2)}) %collective-permute-start.4) | collective-permute-done | bytes 65568 | tf_op jit(solution)/shard_map/ppermute | solution.py:341
  53.5 2.8 %all-gather.1 = bf16[64,2048]{1,0:T(8,128)(2,1)S(1)} all-gather(bf16[32,2048]{1,0:T(8,128)(2,1)S(1)} %pad_maximum_fusion.2), channel_id=3, replica_groups={{0,1},{2,3},{4,5},{6,7},{8,9},{10,11},{12,13},{14,15},{16,17},{18,19},{..., dimensions={0}, use_global_device_ids=true | all-gather | bytes 393216 | tf_op jit(solution)/shard_map/all_gather | solution.py:379
  56.3 0.0 copy-done.1
  56.3 7.1 %backward_planes.1 = bf16[32,16,2048]{2,1,0:T(8,128)(2,1)} custom-call(f32[32]{0:T(128)S(1)} %copy-done.1, bf16[16,2048]{1,0:T(8,128)(2,1)S(1)} %fusion.4.own_ref, bf16[2,32,2048]{2,1,0:T(8,128)(2,1)S(1)} %bitcast.12), custom_call_target="tpu_custom_call" | custom-call | tf_op jit(solution)/shard_map/backward_planes/pallas_call | solution.py:297
  (19 shorter events, 0.3 us)
Async XLA Ops:
  0.6 0.7 %copy-start = (f32[32]{0:T(128)S(1)}, f32[32]{0:T(128)}, u32[]{:S(2)}) copy-start(f32[32]{0:T(128)} %magnify_ref.3) | copy-start | bytes 388
  1.3 9.0 %copy-start.2 = (f32[16,512]{1,0:T(8,128)S(1)}, f32[16,512]{1,0:T(8,128)}, u32[]{:S(2)}) copy-start(f32[16,512]{1,0:T(8,128)} %param.6) | copy-start | bytes 98308
  1.3 9.0 %copy-start.3 = (s32[16,512]{1,0:T(8,128)S(1)}, s32[16,512]{1,0:T(8,128)}, u32[]{:S(2)}) copy-start(s32[16,512]{1,0:T(8,128)} %param.7) | copy-start | bytes 98308
  7.7 3.6 %collective-permute-start = (bf16[32,2048]{1,0:T(8,128)(2,1)S(1)}, bf16[32,2048]{1,0:T(8,128)(2,1)S(1)}, u32[]{:S(2)}, u32[]{:S(2)}) collective-permute-start(bf16[32,2048]{1,0:T(8,128)(2,1)S(1)} %get-tuple-element.8), channel_id=1, source_target_pairs={{0,1},{1,0},{2,3},{3,2},{4,5},{5,4},{6,7},{7,6},{8,9},{9,8},{10,11... | collective-permute-start | bytes 393224 | tf_op jit(solution)/shard_map/ppermute | solution.py:351
  11.3 12.6 %collective-permute-start.1 = (bf16[16,2048]{1,0:T(8,128)(2,1)S(1)}, bf16[16,2048]{1,0:T(8,128)(2,1)S(1)}, u32[]{:S(2)}, u32[]{:S(2)}) collective-permute-start(bf16[16,2048]{1,0:T(8,128)(2,1)S(1)} %get-tuple-element.12), channel_id=1, source_target_pairs={{0,4},{2,6},{4,8},{5,1},{6,10},{7,3},{8,12},{9,5},{10,14},{11,7},{... | collective-permute-start | bytes 196616 | tf_op jit(solution)/shard_map/ppermute | solution.py:341
  21.9 5.9 %collective-permute-start.2 = (bf16[16,2048]{1,0:T(8,128)(2,1)S(1)}, bf16[16,2048]{1,0:T(8,128)(2,1)S(1)}, u32[]{:S(2)}, u32[]{:S(2)}) collective-permute-start(bf16[16,2048]{1,0:T(8,128)(2,1)S(1)} %get-tuple-element.13), channel_id=1, source_target_pairs={{0,8},{2,10},{4,12},{6,14},{8,16},{9,1},{10,18},{11,3},{12,20},{13... | collective-permute-start | bytes 196616 | tf_op jit(solution)/shard_map/ppermute | solution.py:341
  27.8 11.1 %collective-permute-start.3 = (bf16[16,3072]{1,0:T(8,128)(2,1)S(1)}, bf16[16,3072]{1,0:T(8,128)(2,1)S(1)}, u32[]{:S(2)}, u32[]{:S(2)}) collective-permute-start(bf16[16,3072]{1,0:T(8,128)(2,1)S(1)} %pad_maximum_fusion.3), channel_id=1, source_target_pairs={{0,2},{1,3},{2,0},{3,1},{4,6},{5,7},{6,4},{7,5},{8,10},{9,11},{10,... | collective-permute-start | bytes 294920 | tf_op jit(solution)/shard_map/ppermute | solution.py:360
  38.9 17.4 %copy-start.1 = (f32[32]{0:T(128)S(1)}, f32[32]{0:T(128)}, u32[]{:S(2)}) copy-start(f32[32]{0:T(128)} %magnify_ref.3) | copy-start | bytes 388
  41.4 9.5 %collective-permute-start.5 = (bf16[16,2048]{1,0:T(8,128)(2,1)S(1)}, bf16[16,2048]{1,0:T(8,128)(2,1)S(1)}, u32[]{:S(2)}, u32[]{:S(2)}) collective-permute-start(bf16[16,2048]{1,0:T(8,128)(2,1)S(1)} %fusion.4.own_ref), channel_id=1, source_target_pairs={{0,8},{2,10},{4,12},{6,14},{8,16},{9,1},{10,18},{11,3},{12,20},{13... | collective-permute-start | bytes 196616 | tf_op jit(solution)/shard_map/ppermute | solution.py:341
  47.5 6.0 %collective-permute-start.4 = (bf16[16,2048]{1,0:T(8,128)(2,1)S(1)}, bf16[16,2048]{1,0:T(8,128)(2,1)S(1)}, u32[]{:S(2)}, u32[]{:S(2)}) collective-permute-start(bf16[16,2048]{1,0:T(8,128)(2,1)S(1)} %fusion.4.own_ref), channel_id=1, source_target_pairs={{0,4},{2,6},{4,8},{5,1},{6,10},{7,3},{8,12},{9,5},{10,14},{11,7},{... | collective-permute-start | bytes 196616 | tf_op jit(solution)/shard_map/ppermute | solution.py:341

commit v5 on v4

--- a/solution.py
+++ b/solution.py
@@ -84,8 +84,8 @@
 
 
 def forward_kernel(
-    magnify_ref, volume_ref, own_ref, near_ref, far_ref, send_ref,
-    volume, arrival, resampled, row_table, source, low, high,
+    magnify_in, volume_ref, own_ref, near_ref, far_ref, send_ref,
+    magnify_ref, noted, volume, arrival, resampled, row_table, source, low, high,
 ):
     planes, slab_rows, cols = volume_ref.shape
     groups = planes // GROUP
@@ -101,8 +101,11 @@
             volume_ref.at[planes_of], volume.at[planes_of, :, pl.ds(0, cols)], arrival.at[part]
         )
 
+    note = pltpu.make_async_copy(magnify_in, magnify_ref, noted)
+    note.start()
     for part in range(planes // FETCHED):
         fetch(part).start()
+    note.wait()
 
     lane = lax.broadcasted_iota(jnp.int32, (GROUP, LANES), 1)
     row = lax.broadcasted_iota(jnp.int32, (frame_rows, GROUP * slab_rows), 0)
@@ -271,11 +274,13 @@
     run_cols = cols + LANES
     return pl.pallas_call(
         forward_kernel,
-        in_specs=[SMEM, ANY],
+        in_specs=[ANY, ANY],
         out_specs=[VMEM] * 4,
         out_shape=[jax.ShapeDtypeStruct(band, jnp.float32)] * 3
         + [jax.ShapeDtypeStruct(pair, jnp.bfloat16)],
         scratch_shapes=[
+            pltpu.SMEM((planes,), jnp.float32),
+            pltpu.SemaphoreType.DMA(()),
             pltpu.VMEM((planes, slab_rows, run_cols), volume.dtype),
             pltpu.SemaphoreType.DMA((planes // FETCHED,)),
             pltpu.VMEM((groups, GROUP * slab_rows, cols), jnp.bfloat16),
@@ -347,8 +352,10 @@
     cols = own_cols * row_count
 
     pairs = [[q, q + 1] for q in range(0, row_count, 2)]
+    across = [[q, q + 2] for q in range(row_count // 2)]
     own, near, far, send = forward(magnify, volume)
-    got = lax.ppermute(send, "row", [(q, q ^ 1) for q in range(row_count)]).astype(jnp.float32)
+    sent = lax.all_gather(send, "row", axis_index_groups=pairs)
+    got = jnp.where(lax.axis_index("row") % 2 == 0, sent[1], sent[0]).astype(jnp.float32)
     near = both_ways((near + got[:slab_rows]).astype(jnp.bfloat16), 1, True)
     far = both_ways((far + got[slab_rows:]).astype(jnp.bfloat16), 2, True)
     total = own + near.astype(jnp.float32) + far.astype(jnp.float32)
@@ -357,17 +364,20 @@
     fine = (goal - coarse.astype(jnp.float32)).astype(jnp.bfloat16)
     coarse = jnp.where(live_pixels == 0, jnp.bfloat16(DEAD), coarse)
     message = jnp.concatenate([total.astype(jnp.bfloat16), coarse, fine], axis=1)
-    other = lax.ppermute(message, "row", [(q, q ^ 2) for q in range(row_count)])
-    total = total + other[:, :cols].astype(jnp.float32)
-    message = jnp.concatenate([total.astype(jnp.bfloat16), message[:, cols:], other[:, cols:]], axis=1)
+    halves = lax.all_gather(message, "row", axis_index_groups=across)
+    total = halves[0, :, :cols].astype(jnp.float32) + halves[1, :, :cols].astype(jnp.float32)
+    message = jnp.concatenate(
+        [total.astype(jnp.bfloat16), halves[0, :, cols:], halves[1, :, cols:]], axis=1
+    )
     gathered = lax.all_gather(message, "row", axis_index_groups=pairs).astype(jnp.float32)
-    projection = gathered[:, :, :cols].sum(axis=0)
-    lower_half = lax.axis_index("row") < 2
-    mine, others = gathered[:, :, cols : cols + 2 * own_cols], gathered[:, :, cols + 2 * own_cols :]
-    members = [jnp.where(lower_half, mine, others), jnp.where(lower_half, others, mine)]
-    members = [half[core] for half in members for core in range(2)]
-    all_coarse = jnp.concatenate([goals[:, :own_cols] for goals in members], axis=1)
-    all_fine = jnp.concatenate([goals[:, own_cols:] for goals in members], axis=1)
+    projection = gathered[0, :, :cols] + gathered[1, :, :cols]
+    members = [
+        gathered[core, :, cols + 2 * half * own_cols : cols + 2 * (half + 1) * own_cols]
+        for half in range(2)
+        for core in range(2)
+    ]
+    all_coarse = jnp.concatenate([member[:, :own_cols] for member in members], axis=1)
+    all_fine = jnp.concatenate([member[:, own_cols:] for member in members], axis=1)
     residual = jnp.where(
         all_coarse > 0.5 * DEAD, 0.0, projection - (all_coarse + all_fine)
     ).astype(jnp.bfloat16)

time: 63.7 us -> 63 us (0.989)
  blocking collectives: 5.09 us -> 22.3 us
  starting transfers between devices: 31.9 us -> 18.8 us
  waiting for transfers between devices: 10.5 us -> 6.46 us
    all_gather x0 -> x2, blocking collectives: none -> 15 us  [the longest x1 12.7 us: shards(): halves = lax.all_gather(message, 'row', axis_index_groups=across)]
    ppermute x2 -> x0, starting transfers between devices: 10.5 us -> none  [the longest x1 7.94 us: shards(): other = lax.ppermute(message, 'row', [(q, q ^ 2) for q in range(row_count)])]
    ppermute x2 -> x0, waiting for transfers between devices: 4.02 us -> none  [the longest x1 3.1 us: shards(): other = lax.ppermute(message, 'row', [(q, q ^ 2) for q in range(row_count)])]
    ppermute x4, starting transfers between devices: 21.4 us -> 18.8 us  [both_ways(): return lax.ppermute(block, ('slab', 'row'), route)]
    all_gather x1, blocking collectives: 2.83 us -> 5.25 us  [shards(): halo = lax.all_gather(arrived, 'row', axis_index_groups=pairs)]
  transfers between devices with their start and end apart: 6 -> 4, of which waited for: 4 -> 2; matrix products, arithmetic and copies ran while one was open for 1% -> 1% of each run, Pallas kernels for 0% -> 0%
where the time goes in v5:
time: 63 us; the launch traced here: 62.8 us
  blocking collectives  22.3 us (35%)
  starting transfers between devices  18.8 us (30%)
  Pallas kernels  12.9 us (20%)
  waiting for transfers between devices  6.46 us (10%)
  local copies, waits for them, and re-layouts  1.34 us (2%)
  between operations  0.82 us (1%)
    ppermute x4, starting transfers between devices, both_ways(): return lax.ppermute(block, ('slab', 'row'), route)  18.8 us
    all_gather x1, blocking collectives, shards(): halves = lax.all_gather(message, 'row', axis_index_groups=across)  12.7 us
    pallas_call x1, Pallas kernels, backward(): pl.pallas_call(backward_kernel, in_specs=[SMEM, VMEM, VMEM], out_specs=AN...  7.06 us
    ppermute x4, waiting for transfers between devices, both_ways(): return lax.ppermute(block, ('slab', 'row'), route)  6.46 us
    pallas_call x1, Pallas kernels, forward(): pl.pallas_call(forward_kernel, in_specs=[ANY, ANY], out_specs=[VMEM] * 4,...  5.82 us
    all_gather x1, blocking collectives, shards(): halo = lax.all_gather(arrived, 'row', axis_index_groups=pairs)  5.25 us
    all_gather x1, blocking collectives, shards(): sent = lax.all_gather(send, 'row', axis_index_groups=pairs)  2.32 us
    all_gather x1, blocking collectives, shards(): lax.all_gather(message, 'row', axis_index_groups=pairs).astype(jnp.float32)  1.99 us
  transfers between devices with their start and end apart: 4, of which 2 were waited for; matrix products, arithmetic and copies ran while one was open for 1% of the time, Pallas kernels for 0%

profile of v5, /device:TPU:57, one launch (start us, length us, event | category | flops | bytes accessed | tf_op | source)
XLA Modules:
  0.0 62.8 jit_solution(12921777188889493700)
XLA Ops:
  0.6 0.0 copy-start
  0.7 0.6 %copy-done = f32[32]{0:T(128)S(1)} copy-done((f32[32]{0:T(128)S(1)}, f32[32]{0:T(128)}, u32[]{:S(2)}) %copy-start) | copy-done | bytes 152
  1.3 0.0 copy-start.2
  1.3 0.0 copy-start.3
  1.3 5.8 %forward_planes.1 = (f32[16,2048]{1,0:T(8,128)S(1)}, f32[16,2048]{1,0:T(8,128)S(1)}, f32[16,2048]{1,0:T(8,128)S(1)}, bf16[32,2048]{1,0:T(8,128)(2,1)S(1)}) custom-call(f32[32]{0:T(128)S(1)} %copy-done, bf16[32,16,2048]{2,1,0:T(8,128)(2,1)} %volume_ref.1), custom_call_target="tpu_custom_call" | custom-call | tf_op jit(solution)/shard_map/forward_planes/pallas_call | solution.py:275
  7.1 2.3 %all-gather = bf16[64,2048]{1,0:T(8,128)(2,1)S(1)} all-gather(bf16[32,2048]{1,0:T(8,128)(2,1)S(1)} %get-tuple-element.8), channel_id=2, replica_groups={{0,1},{2,3},{4,5},{6,7},{8,9},{10,11},{12,13},{14,15},{16,17},{18,19},{..., dimensions={0}, use_global_device_ids=true | all-gather | bytes 393216 | tf_op jit(solution)/shard_map/all_gather | solution.py:357
  9.5 10.6 %collective-permute-start = (bf16[16,2048]{1,0:T(8,128)(2,1)S(1)}, bf16[16,2048]{1,0:T(8,128)(2,1)S(1)}, u32[]{:S(2)}, u32[]{:S(2)}) collective-permute-start(bf16[16,2048]{1,0:T(8,128)(2,1)S(1)} %get-tuple-element.16), channel_id=1, source_target_pairs={{0,4},{2,6},{4,8},{5,1},{6,10},{7,3},{8,12},{9,5},{10,14},{11,7},{... | collective-permute-start | bytes 196616 | tf_op jit(solution)/shard_map/ppermute | solution.py:346
  20.1 1.9 %collective-permute-start.1 = (bf16[16,2048]{1,0:T(8,128)(2,1)S(1)}, bf16[16,2048]{1,0:T(8,128)(2,1)S(1)}, u32[]{:S(2)}, u32[]{:S(2)}) collective-permute-start(bf16[16,2048]{1,0:T(8,128)(2,1)S(1)} %get-tuple-element.17), channel_id=1, source_target_pairs={{0,8},{2,10},{4,12},{6,14},{8,16},{9,1},{10,18},{11,3},{12,20},{13... | collective-permute-start | bytes 196616 | tf_op jit(solution)/shard_map/ppermute | solution.py:346
  22.0 0.0 copy-done.2
  22.1 0.0 copy-done.3
  22.1 0.0 collective-permute-done
  22.1 3.9 %collective-permute-done.1 = bf16[16,2048]{1,0:T(8,128)(2,1)S(1)} collective-permute-done((bf16[16,2048]{1,0:T(8,128)(2,1)S(1)}, bf16[16,2048]{1,0:T(8,128)(2,1)S(1)}, u32[]{:S(2)}, u32[]{:S(2)}) %collective-permute-start.1) | collective-permute-done | bytes 65568 | tf_op jit(solution)/shard_map/ppermute | solution.py:346
  26.1 12.7 %all-gather.1 = bf16[32,3072]{1,0:T(8,128)(2,1)S(1)} all-gather(bf16[16,3072]{1,0:T(8,128)(2,1)S(1)} %pad_maximum_fusion.3), channel_id=3, replica_groups={{0,2},{1,3},{4,6},{5,7},{8,10},{9,11},{12,14},{13,15},{16,18},{17,19},{..., dimensions={0}, use_global_device_ids=true | all-gather | bytes 294912 | tf_op jit(solution)/shard_map/all_gather | solution.py:367
  38.8 0.0 copy-start.1
  38.9 2.0 %all-gather.2 = bf16[32,4096]{1,0:T(8,128)(2,1)S(1)} all-gather(bf16[16,4096]{1,0:T(8,128)(2,1)S(1)} %pad_maximum_fusion), channel_id=4, replica_groups={{0,1},{2,3},{4,5},{6,7},{8,9},{10,11},{12,13},{14,15},{16,17},{18,19},{..., dimensions={0}, use_global_device_ids=true | all-gather | bytes 393216 | tf_op jit(solution)/shard_map/all_gather | solution.py:372
  41.0 3.4 %collective-permute-start.3 = (bf16[16,2048]{1,0:T(8,128)(2,1)S(1)}, bf16[16,2048]{1,0:T(8,128)(2,1)S(1)}, u32[]{:S(2)}, u32[]{:S(2)}) collective-permute-start(bf16[16,2048]{1,0:T(8,128)(2,1)S(1)} %get-tuple-element.10.own_ref), channel_id=1, source_target_pairs={{0,8},{2,10},{4,12},{6,14},{8,16},{9,1},{10,18},{11,3},{12,20},{13... | collective-permute-start | bytes 196616 | tf_op jit(solution)/shard_map/ppermute | solution.py:346
  44.4 2.8 %collective-permute-start.2 = (bf16[16,2048]{1,0:T(8,128)(2,1)S(1)}, bf16[16,2048]{1,0:T(8,128)(2,1)S(1)}, u32[]{:S(2)}, u32[]{:S(2)}) collective-permute-start(bf16[16,2048]{1,0:T(8,128)(2,1)S(1)} %get-tuple-element.10.own_ref), channel_id=1, source_target_pairs={{0,4},{2,6},{4,8},{5,1},{6,10},{7,3},{8,12},{9,5},{10,14},{11,7},{... | collective-permute-start | bytes 196616 | tf_op jit(solution)/shard_map/ppermute | solution.py:346
  47.3 0.6 dynamic-slice_bitcast_fusion
  47.9 0.0 collective-permute-done.3
  47.9 2.5 %collective-permute-done.2 = bf16[16,2048]{1,0:T(8,128)(2,1)S(1)} collective-permute-done((bf16[16,2048]{1,0:T(8,128)(2,1)S(1)}, bf16[16,2048]{1,0:T(8,128)(2,1)S(1)}, u32[]{:S(2)}, u32[]{:S(2)}) %collective-permute-start.2) | collective-permute-done | bytes 65568 | tf_op jit(solution)/shard_map/ppermute | solution.py:346
  50.4 5.3 %all-gather.3 = bf16[64,2048]{1,0:T(8,128)(2,1)S(1)} all-gather(bf16[32,2048]{1,0:T(8,128)(2,1)S(1)} %pad_maximum_fusion.2), channel_id=5, replica_groups={{0,1},{2,3},{4,5},{6,7},{8,9},{10,11},{12,13},{14,15},{16,17},{18,19},{..., dimensions={0}, use_global_device_ids=true | all-gather | bytes 393216 | tf_op jit(solution)/shard_map/all_gather | solution.py:389
  55.7 0.0 copy-done.1
  55.7 7.1 %backward_planes.1 = bf16[32,16,2048]{2,1,0:T(8,128)(2,1)} custom-call(f32[32]{0:T(128)S(1)} %copy-done.1, bf16[16,2048]{1,0:T(8,128)(2,1)S(1)} %get-tuple-element.10.own_ref, bf16[2,32,2048]{2,1,0:T(8,128)(2,1)S(1)} %bitcast.39), custom_call_target="tpu_custom_call" | custom-call | tf_op jit(solution)/shard_map/backward_planes/pallas_call | solution.py:302
  (15 shorter events, 0.3 us)
Async XLA Ops:
  0.6 0.7 %copy-start = (f32[32]{0:T(128)S(1)}, f32[32]{0:T(128)}, u32[]{:S(2)}) copy-start(f32[32]{0:T(128)} %magnify_ref.1) | copy-start | bytes 388
  1.3 20.7 %copy-start.2 = (f32[16,512]{1,0:T(8,128)S(1)}, f32[16,512]{1,0:T(8,128)}, u32[]{:S(2)}) copy-start(f32[16,512]{1,0:T(8,128)} %param.6) | copy-start | bytes 98308
  1.3 20.8 %copy-start.3 = (s32[16,512]{1,0:T(8,128)S(1)}, s32[16,512]{1,0:T(8,128)}, u32[]{:S(2)}) copy-start(s32[16,512]{1,0:T(8,128)} %param.7) | copy-start | bytes 98308
  9.5 12.6 %collective-permute-start = (bf16[16,2048]{1,0:T(8,128)(2,1)S(1)}, bf16[16,2048]{1,0:T(8,128)(2,1)S(1)}, u32[]{:S(2)}, u32[]{:S(2)}) collective-permute-start(bf16[16,2048]{1,0:T(8,128)(2,1)S(1)} %get-tuple-element.16), channel_id=1, source_target_pairs={{0,4},{2,6},{4,8},{5,1},{6,10},{7,3},{8,12},{9,5},{10,14},{11,7},{... | collective-permute-start | bytes 196616 | tf_op jit(solution)/shard_map/ppermute | solution.py:346
  20.1 5.9 %collective-permute-start.1 = (bf16[16,2048]{1,0:T(8,128)(2,1)S(1)}, bf16[16,2048]{1,0:T(8,128)(2,1)S(1)}, u32[]{:S(2)}, u32[]{:S(2)}) collective-permute-start(bf16[16,2048]{1,0:T(8,128)(2,1)S(1)} %get-tuple-element.17), channel_id=1, source_target_pairs={{0,8},{2,10},{4,12},{6,14},{8,16},{9,1},{10,18},{11,3},{12,20},{13... | collective-permute-start | bytes 196616 | tf_op jit(solution)/shard_map/ppermute | solution.py:346
  38.8 16.9 %copy-start.1 = (f32[32]{0:T(128)S(1)}, f32[32]{0:T(128)}, u32[]{:S(2)}) copy-start(f32[32]{0:T(128)} %magnify_ref.1) | copy-start | bytes 388
  41.0 6.9 %collective-permute-start.3 = (bf16[16,2048]{1,0:T(8,128)(2,1)S(1)}, bf16[16,2048]{1,0:T(8,128)(2,1)S(1)}, u32[]{:S(2)}, u32[]{:S(2)}) collective-permute-start(bf16[16,2048]{1,0:T(8,128)(2,1)S(1)} %get-tuple-element.10.own_ref), channel_id=1, source_target_pairs={{0,8},{2,10},{4,12},{6,14},{8,16},{9,1},{10,18},{11,3},{12,20},{13... | collective-permute-start | bytes 196616 | tf_op jit(solution)/shard_map/ppermute | solution.py:346
  44.4 6.0 %collective-permute-start.2 = (bf16[16,2048]{1,0:T(8,128)(2,1)S(1)}, bf16[16,2048]{1,0:T(8,128)(2,1)S(1)}, u32[]{:S(2)}, u32[]{:S(2)}) collective-permute-start(bf16[16,2048]{1,0:T(8,128)(2,1)S(1)} %get-tuple-element.10.own_ref), channel_id=1, source_target_pairs={{0,4},{2,6},{4,8},{5,1},{6,10},{7,3},{8,12},{9,5},{10,14},{11,7},{... | collective-permute-start | bytes 196616 | tf_op jit(solution)/shard_map/ppermute | solution.py:346

commit v6 on v5

--- a/solution.py
+++ b/solution.py
@@ -159,7 +159,7 @@
                 before = run
         return carry
 
-    lax.fori_loop(0, groups, group_step, 0)
+    lax.fori_loop(0, groups, group_step, 0, unroll=True)
 
     upward = lax.axis_index("row") % 2 == 0
     r = slab_rows

time: 63 us -> 62.4 us (level)
  no operation moved by 1% of the time
where the time goes in v6:
time: 62.4 us; the launch traced here: 62.1 us
  blocking collectives  22.2 us (36%)
  starting transfers between devices  18.8 us (30%)
  Pallas kernels  12.3 us (20%)
  waiting for transfers between devices  6.46 us (10%)
  local copies, waits for them, and re-layouts  1.34 us (2%)
  between operations  0.82 us (1%)
    ppermute x4, starting transfers between devices, both_ways(): return lax.ppermute(block, ('slab', 'row'), route)  18.8 us
    all_gather x1, blocking collectives, shards(): halves = lax.all_gather(message, 'row', axis_index_groups=across)  12.7 us
    pallas_call x1, Pallas kernels, backward(): pl.pallas_call(backward_kernel, in_specs=[SMEM, VMEM, VMEM], out_specs=AN...  7.06 us
    ppermute x4, waiting for transfers between devices, both_ways(): return lax.ppermute(block, ('slab', 'row'), route)  6.46 us
    all_gather x1, blocking collectives, shards(): halo = lax.all_gather(arrived, 'row', axis_index_groups=pairs)  5.25 us
    pallas_call x1, Pallas kernels, forward(): pl.pallas_call(forward_kernel, in_specs=[ANY, ANY], out_specs=[VMEM] * 4,...  5.23 us
    all_gather x1, blocking collectives, shards(): sent = lax.all_gather(send, 'row', axis_index_groups=pairs)  2.31 us
    all_gather x1, blocking collectives, shards(): lax.all_gather(message, 'row', axis_index_groups=pairs).astype(jnp.float32)  1.99 us
  transfers between devices with their start and end apart: 4, of which 2 were waited for; matrix products, arithmetic and copies ran while one was open for 1% of the time, Pallas kernels for 0%

profile of v6, /device:TPU:57, one launch (start us, length us, event | category | flops | bytes accessed | tf_op | source)
XLA Modules:
  0.0 62.1 jit_solution(17572582278715605817)
XLA Ops:
  0.6 0.0 copy-start
  0.7 0.6 %copy-done = f32[32]{0:T(128)S(1)} copy-done((f32[32]{0:T(128)S(1)}, f32[32]{0:T(128)}, u32[]{:S(2)}) %copy-start) | copy-done | bytes 152
  1.3 0.0 copy-start.2
  1.3 0.0 copy-start.3
  1.3 5.2 %forward_planes.1 = (f32[16,2048]{1,0:T(8,128)S(1)}, f32[16,2048]{1,0:T(8,128)S(1)}, f32[16,2048]{1,0:T(8,128)S(1)}, bf16[32,2048]{1,0:T(8,128)(2,1)S(1)}) custom-call(f32[32]{0:T(128)S(1)} %copy-done, bf16[32,16,2048]{2,1,0:T(8,128)(2,1)} %volume_ref.1), custom_call_target="tpu_custom_call" | custom-call | tf_op jit(solution)/shard_map/forward_planes/pallas_call | solution.py:275
  6.5 2.3 %all-gather = bf16[64,2048]{1,0:T(8,128)(2,1)S(1)} all-gather(bf16[32,2048]{1,0:T(8,128)(2,1)S(1)} %get-tuple-element.8), channel_id=2, replica_groups={{0,1},{2,3},{4,5},{6,7},{8,9},{10,11},{12,13},{14,15},{16,17},{18,19},{..., dimensions={0}, use_global_device_ids=true | all-gather | bytes 393216 | tf_op jit(solution)/shard_map/all_gather | solution.py:357
  8.9 10.6 %collective-permute-start = (bf16[16,2048]{1,0:T(8,128)(2,1)S(1)}, bf16[16,2048]{1,0:T(8,128)(2,1)S(1)}, u32[]{:S(2)}, u32[]{:S(2)}) collective-permute-start(bf16[16,2048]{1,0:T(8,128)(2,1)S(1)} %get-tuple-element.16), channel_id=1, source_target_pairs={{0,4},{2,6},{4,8},{5,1},{6,10},{7,3},{8,12},{9,5},{10,14},{11,7},{... | collective-permute-start | bytes 196616 | tf_op jit(solution)/shard_map/ppermute | solution.py:346
  19.5 1.9 %collective-permute-start.1 = (bf16[16,2048]{1,0:T(8,128)(2,1)S(1)}, bf16[16,2048]{1,0:T(8,128)(2,1)S(1)}, u32[]{:S(2)}, u32[]{:S(2)}) collective-permute-start(bf16[16,2048]{1,0:T(8,128)(2,1)S(1)} %get-tuple-element.17), channel_id=1, source_target_pairs={{0,8},{2,10},{4,12},{6,14},{8,16},{9,1},{10,18},{11,3},{12,20},{13... | collective-permute-start | bytes 196616 | tf_op jit(solution)/shard_map/ppermute | solution.py:346
  21.4 0.0 copy-done.2
  21.5 0.0 copy-done.3
  21.5 0.0 collective-permute-done
  21.5 3.9 %collective-permute-done.1 = bf16[16,2048]{1,0:T(8,128)(2,1)S(1)} collective-permute-done((bf16[16,2048]{1,0:T(8,128)(2,1)S(1)}, bf16[16,2048]{1,0:T(8,128)(2,1)S(1)}, u32[]{:S(2)}, u32[]{:S(2)}) %collective-permute-start.1) | collective-permute-done | bytes 65568 | tf_op jit(solution)/shard_map/ppermute | solution.py:346
  25.5 12.7 %all-gather.1 = bf16[32,3072]{1,0:T(8,128)(2,1)S(1)} all-gather(bf16[16,3072]{1,0:T(8,128)(2,1)S(1)} %pad_maximum_fusion.3), channel_id=3, replica_groups={{0,2},{1,3},{4,6},{5,7},{8,10},{9,11},{12,14},{13,15},{16,18},{17,19},{..., dimensions={0}, use_global_device_ids=true | all-gather | bytes 294912 | tf_op jit(solution)/shard_map/all_gather | solution.py:367
  38.2 0.0 copy-start.1
  38.2 2.0 %all-gather.2 = bf16[32,4096]{1,0:T(8,128)(2,1)S(1)} all-gather(bf16[16,4096]{1,0:T(8,128)(2,1)S(1)} %pad_maximum_fusion), channel_id=4, replica_groups={{0,1},{2,3},{4,5},{6,7},{8,9},{10,11},{12,13},{14,15},{16,17},{18,19},{..., dimensions={0}, use_global_device_ids=true | all-gather | bytes 393216 | tf_op jit(solution)/shard_map/all_gather | solution.py:372
  40.4 3.4 %collective-permute-start.3 = (bf16[16,2048]{1,0:T(8,128)(2,1)S(1)}, bf16[16,2048]{1,0:T(8,128)(2,1)S(1)}, u32[]{:S(2)}, u32[]{:S(2)}) collective-permute-start(bf16[16,2048]{1,0:T(8,128)(2,1)S(1)} %get-tuple-element.10.own_ref), channel_id=1, source_target_pairs={{0,8},{2,10},{4,12},{6,14},{8,16},{9,1},{10,18},{11,3},{12,20},{13... | collective-permute-start | bytes 196616 | tf_op jit(solution)/shard_map/ppermute | solution.py:346
  43.8 2.8 %collective-permute-start.2 = (bf16[16,2048]{1,0:T(8,128)(2,1)S(1)}, bf16[16,2048]{1,0:T(8,128)(2,1)S(1)}, u32[]{:S(2)}, u32[]{:S(2)}) collective-permute-start(bf16[16,2048]{1,0:T(8,128)(2,1)S(1)} %get-tuple-element.10.own_ref), channel_id=1, source_target_pairs={{0,4},{2,6},{4,8},{5,1},{6,10},{7,3},{8,12},{9,5},{10,14},{11,7},{... | collective-permute-start | bytes 196616 | tf_op jit(solution)/shard_map/ppermute | solution.py:346
  46.7 0.6 %dynamic-slice_bitcast_fusion = f32[16,512]{1,0:T(8,128)} fusion(f32[1,16,2048]{2,1,0:T(8,128)S(1)} %get-tuple-element.11, s32[]{:T(128)S(6)} %select_n.31), kind=kLoop, calls=%fused_computation.27 | loop fusion | bytes 65540 | tf_op jit(solution)/shard_map/dynamic_slice | solution.py:384
  47.3 0.0 collective-permute-done.3
  47.3 2.5 %collective-permute-done.2 = bf16[16,2048]{1,0:T(8,128)(2,1)S(1)} collective-permute-done((bf16[16,2048]{1,0:T(8,128)(2,1)S(1)}, bf16[16,2048]{1,0:T(8,128)(2,1)S(1)}, u32[]{:S(2)}, u32[]{:S(2)}) %collective-permute-start.2) | collective-permute-done | bytes 65568 | tf_op jit(solution)/shard_map/ppermute | solution.py:346
  49.8 5.2 %all-gather.3 = bf16[64,2048]{1,0:T(8,128)(2,1)S(1)} all-gather(bf16[32,2048]{1,0:T(8,128)(2,1)S(1)} %pad_maximum_fusion.2), channel_id=5, replica_groups={{0,1},{2,3},{4,5},{6,7},{8,9},{10,11},{12,13},{14,15},{16,17},{18,19},{..., dimensions={0}, use_global_device_ids=true | all-gather | bytes 393216 | tf_op jit(solution)/shard_map/all_gather | solution.py:389
  55.1 0.0 copy-done.1
  55.1 7.1 %backward_planes.1 = bf16[32,16,2048]{2,1,0:T(8,128)(2,1)} custom-call(f32[32]{0:T(128)S(1)} %copy-done.1, bf16[16,2048]{1,0:T(8,128)(2,1)S(1)} %get-tuple-element.10.own_ref, bf16[2,32,2048]{2,1,0:T(8,128)(2,1)S(1)} %bitcast.39), custom_call_target="tpu_custom_call" | custom-call | tf_op jit(solution)/shard_map/backward_planes/pallas_call | solution.py:302
  (15 shorter events, 0.3 us)
Async XLA Ops:
  0.6 0.7 %copy-start = (f32[32]{0:T(128)S(1)}, f32[32]{0:T(128)}, u32[]{:S(2)}) copy-start(f32[32]{0:T(128)} %magnify_ref.1) | copy-start | bytes 388
  1.3 20.1 %copy-start.2 = (f32[16,512]{1,0:T(8,128)S(1)}, f32[16,512]{1,0:T(8,128)}, u32[]{:S(2)}) copy-start(f32[16,512]{1,0:T(8,128)} %param.6) | copy-start | bytes 98308
  1.3 20.2 %copy-start.3 = (s32[16,512]{1,0:T(8,128)S(1)}, s32[16,512]{1,0:T(8,128)}, u32[]{:S(2)}) copy-start(s32[16,512]{1,0:T(8,128)} %param.7) | copy-start | bytes 98308
  8.9 12.6 %collective-permute-start = (bf16[16,2048]{1,0:T(8,128)(2,1)S(1)}, bf16[16,2048]{1,0:T(8,128)(2,1)S(1)}, u32[]{:S(2)}, u32[]{:S(2)}) collective-permute-start(bf16[16,2048]{1,0:T(8,128)(2,1)S(1)} %get-tuple-element.16), channel_id=1, source_target_pairs={{0,4},{2,6},{4,8},{5,1},{6,10},{7,3},{8,12},{9,5},{10,14},{11,7},{... | collective-permute-start | bytes 196616 | tf_op jit(solution)/shard_map/ppermute | solution.py:346
  19.5 5.9 %collective-permute-start.1 = (bf16[16,2048]{1,0:T(8,128)(2,1)S(1)}, bf16[16,2048]{1,0:T(8,128)(2,1)S(1)}, u32[]{:S(2)}, u32[]{:S(2)}) collective-permute-start(bf16[16,2048]{1,0:T(8,128)(2,1)S(1)} %get-tuple-element.17), channel_id=1, source_target_pairs={{0,8},{2,10},{4,12},{6,14},{8,16},{9,1},{10,18},{11,3},{12,20},{13... | collective-permute-start | bytes 196616 | tf_op jit(solution)/shard_map/ppermute | solution.py:346
  38.2 16.9 %copy-start.1 = (f32[32]{0:T(128)S(1)}, f32[32]{0:T(128)}, u32[]{:S(2)}) copy-start(f32[32]{0:T(128)} %magnify_ref.1) | copy-start | bytes 388
  40.4 6.9 %collective-permute-start.3 = (bf16[16,2048]{1,0:T(8,128)(2,1)S(1)}, bf16[16,2048]{1,0:T(8,128)(2,1)S(1)}, u32[]{:S(2)}, u32[]{:S(2)}) collective-permute-start(bf16[16,2048]{1,0:T(8,128)(2,1)S(1)} %get-tuple-element.10.own_ref), channel_id=1, source_target_pairs={{0,8},{2,10},{4,12},{6,14},{8,16},{9,1},{10,18},{11,3},{12,20},{13... | collective-permute-start | bytes 196616 | tf_op jit(solution)/shard_map/ppermute | solution.py:346
  43.8 6.0 %collective-permute-start.2 = (bf16[16,2048]{1,0:T(8,128)(2,1)S(1)}, bf16[16,2048]{1,0:T(8,128)(2,1)S(1)}, u32[]{:S(2)}, u32[]{:S(2)}) collective-permute-start(bf16[16,2048]{1,0:T(8,128)(2,1)S(1)} %get-tuple-element.10.own_ref), channel_id=1, source_target_pairs={{0,4},{2,6},{4,8},{5,1},{6,10},{7,3},{8,12},{9,5},{10,14},{11,7},{... | collective-permute-start | bytes 196616 | tf_op jit(solution)/shard_map/ppermute | solution.py:346

commit v7 on v6

--- a/solution.py
+++ b/solution.py
@@ -12,7 +12,7 @@
 FIXED_BITS = 16
 FIXED = float(1 << FIXED_BITS)
 GROUP = 8
-SENT = 4
+SENT = 2
 FETCHED = 8
 RUN = 121
 DEAD = 1e30

time: 62.4 us -> 62.4 us (level)
  no operation moved by 1% of the time
where the time goes in v7:
time: 62.4 us; the launch traced here: 62.2 us
  blocking collectives  22.2 us (36%)
  starting transfers between devices  18.8 us (30%)
  Pallas kernels  12.3 us (20%)
  waiting for transfers between devices  6.46 us (10%)
  local copies, waits for them, and re-layouts  1.34 us (2%)
  between operations  0.82 us (1%)
    ppermute x4, starting transfers between devices, both_ways(): return lax.ppermute(block, ('slab', 'row'), route)  18.8 us
    all_gather x1, blocking collectives, shards(): halves = lax.all_gather(message, 'row', axis_index_groups=across)  12.7 us
    pallas_call x1, Pallas kernels, backward(): pl.pallas_call(backward_kernel, in_specs=[SMEM, VMEM, VMEM], out_specs=AN...  7.09 us
    ppermute x4, waiting for transfers between devices, both_ways(): return lax.ppermute(block, ('slab', 'row'), route)  6.46 us
    all_gather x1, blocking collectives, shards(): halo = lax.all_gather(arrived, 'row', axis_index_groups=pairs)  5.25 us
    pallas_call x1, Pallas kernels, forward(): pl.pallas_call(forward_kernel, in_specs=[ANY, ANY], out_specs=[VMEM] * 4,...  5.23 us
    all_gather x1, blocking collectives, shards(): sent = lax.all_gather(send, 'row', axis_index_groups=pairs)  2.31 us
    all_gather x1, blocking collectives, shards(): lax.all_gather(message, 'row', axis_index_groups=pairs).astype(jnp.float32)  1.99 us
  transfers between devices with their start and end apart: 4, of which 2 were waited for; matrix products, arithmetic and copies ran while one was open for 1% of the time, Pallas kernels for 0%

profile of v7, /device:TPU:57, one launch (start us, length us, event | category | flops | bytes accessed | tf_op | source)
XLA Modules:
  0.0 62.2 jit_solution(5463099275214586255)
XLA Ops:
  0.6 0.0 copy-start
  0.7 0.6 %copy-done = f32[32]{0:T(128)S(1)} copy-done((f32[32]{0:T(128)S(1)}, f32[32]{0:T(128)}, u32[]{:S(2)}) %copy-start) | copy-done | bytes 152
  1.3 0.0 copy-start.2
  1.3 0.0 copy-start.3
  1.3 5.2 %forward_planes.1 = (f32[16,2048]{1,0:T(8,128)S(1)}, f32[16,2048]{1,0:T(8,128)S(1)}, f32[16,2048]{1,0:T(8,128)S(1)}, bf16[32,2048]{1,0:T(8,128)(2,1)S(1)}) custom-call(f32[32]{0:T(128)S(1)} %copy-done, bf16[32,16,2048]{2,1,0:T(8,128)(2,1)} %volume_ref.1), custom_call_target="tpu_custom_call" | custom-call | tf_op jit(solution)/shard_map/forward_planes/pallas_call | solution.py:275
  6.5 2.3 %all-gather = bf16[64,2048]{1,0:T(8,128)(2,1)S(1)} all-gather(bf16[32,2048]{1,0:T(8,128)(2,1)S(1)} %get-tuple-element.8), channel_id=2, replica_groups={{0,1},{2,3},{4,5},{6,7},{8,9},{10,11},{12,13},{14,15},{16,17},{18,19},{..., dimensions={0}, use_global_device_ids=true | all-gather | bytes 393216 | tf_op jit(solution)/shard_map/all_gather | solution.py:357
  8.9 10.6 %collective-permute-start = (bf16[16,2048]{1,0:T(8,128)(2,1)S(1)}, bf16[16,2048]{1,0:T(8,128)(2,1)S(1)}, u32[]{:S(2)}, u32[]{:S(2)}) collective-permute-start(bf16[16,2048]{1,0:T(8,128)(2,1)S(1)} %get-tuple-element.16), channel_id=1, source_target_pairs={{0,4},{2,6},{4,8},{5,1},{6,10},{7,3},{8,12},{9,5},{10,14},{11,7},{... | collective-permute-start | bytes 196616 | tf_op jit(solution)/shard_map/ppermute | solution.py:346
  19.5 1.9 %collective-permute-start.1 = (bf16[16,2048]{1,0:T(8,128)(2,1)S(1)}, bf16[16,2048]{1,0:T(8,128)(2,1)S(1)}, u32[]{:S(2)}, u32[]{:S(2)}) collective-permute-start(bf16[16,2048]{1,0:T(8,128)(2,1)S(1)} %get-tuple-element.17), channel_id=1, source_target_pairs={{0,8},{2,10},{4,12},{6,14},{8,16},{9,1},{10,18},{11,3},{12,20},{13... | collective-permute-start | bytes 196616 | tf_op jit(solution)/shard_map/ppermute | solution.py:346
  21.4 0.0 copy-done.2
  21.5 0.0 copy-done.3
  21.5 0.0 collective-permute-done
  21.5 3.9 %collective-permute-done.1 = bf16[16,2048]{1,0:T(8,128)(2,1)S(1)} collective-permute-done((bf16[16,2048]{1,0:T(8,128)(2,1)S(1)}, bf16[16,2048]{1,0:T(8,128)(2,1)S(1)}, u32[]{:S(2)}, u32[]{:S(2)}) %collective-permute-start.1) | collective-permute-done | bytes 65568 | tf_op jit(solution)/shard_map/ppermute | solution.py:346
  25.5 12.7 %all-gather.1 = bf16[32,3072]{1,0:T(8,128)(2,1)S(1)} all-gather(bf16[16,3072]{1,0:T(8,128)(2,1)S(1)} %pad_maximum_fusion.3), channel_id=3, replica_groups={{0,2},{1,3},{4,6},{5,7},{8,10},{9,11},{12,14},{13,15},{16,18},{17,19},{..., dimensions={0}, use_global_device_ids=true | all-gather | bytes 294912 | tf_op jit(solution)/shard_map/all_gather | solution.py:367
  38.2 0.0 copy-start.1
  38.2 2.0 %all-gather.2 = bf16[32,4096]{1,0:T(8,128)(2,1)S(1)} all-gather(bf16[16,4096]{1,0:T(8,128)(2,1)S(1)} %pad_maximum_fusion), channel_id=4, replica_groups={{0,1},{2,3},{4,5},{6,7},{8,9},{10,11},{12,13},{14,15},{16,17},{18,19},{..., dimensions={0}, use_global_device_ids=true | all-gather | bytes 393216 | tf_op jit(solution)/shard_map/all_gather | solution.py:372
  40.4 3.4 %collective-permute-start.3 = (bf16[16,2048]{1,0:T(8,128)(2,1)S(1)}, bf16[16,2048]{1,0:T(8,128)(2,1)S(1)}, u32[]{:S(2)}, u32[]{:S(2)}) collective-permute-start(bf16[16,2048]{1,0:T(8,128)(2,1)S(1)} %get-tuple-element.10.own_ref), channel_id=1, source_target_pairs={{0,8},{2,10},{4,12},{6,14},{8,16},{9,1},{10,18},{11,3},{12,20},{13... | collective-permute-start | bytes 196616 | tf_op jit(solution)/shard_map/ppermute | solution.py:346
  43.8 2.8 %collective-permute-start.2 = (bf16[16,2048]{1,0:T(8,128)(2,1)S(1)}, bf16[16,2048]{1,0:T(8,128)(2,1)S(1)}, u32[]{:S(2)}, u32[]{:S(2)}) collective-permute-start(bf16[16,2048]{1,0:T(8,128)(2,1)S(1)} %get-tuple-element.10.own_ref), channel_id=1, source_target_pairs={{0,4},{2,6},{4,8},{5,1},{6,10},{7,3},{8,12},{9,5},{10,14},{11,7},{... | collective-permute-start | bytes 196616 | tf_op jit(solution)/shard_map/ppermute | solution.py:346
  46.7 0.6 %dynamic-slice_bitcast_fusion = f32[16,512]{1,0:T(8,128)} fusion(f32[1,16,2048]{2,1,0:T(8,128)S(1)} %get-tuple-element.11, s32[]{:T(128)S(6)} %select_n.31), kind=kLoop, calls=%fused_computation.27 | loop fusion | bytes 65540 | tf_op jit(solution)/shard_map/dynamic_slice | solution.py:384
  47.3 0.0 collective-permute-done.3
  47.3 2.5 %collective-permute-done.2 = bf16[16,2048]{1,0:T(8,128)(2,1)S(1)} collective-permute-done((bf16[16,2048]{1,0:T(8,128)(2,1)S(1)}, bf16[16,2048]{1,0:T(8,128)(2,1)S(1)}, u32[]{:S(2)}, u32[]{:S(2)}) %collective-permute-start.2) | collective-permute-done | bytes 65568 | tf_op jit(solution)/shard_map/ppermute | solution.py:346
  49.8 5.2 %all-gather.3 = bf16[64,2048]{1,0:T(8,128)(2,1)S(1)} all-gather(bf16[32,2048]{1,0:T(8,128)(2,1)S(1)} %pad_maximum_fusion.2), channel_id=5, replica_groups={{0,1},{2,3},{4,5},{6,7},{8,9},{10,11},{12,13},{14,15},{16,17},{18,19},{..., dimensions={0}, use_global_device_ids=true | all-gather | bytes 393216 | tf_op jit(solution)/shard_map/all_gather | solution.py:389
  55.1 0.0 copy-done.1
  55.1 7.1 %backward_planes.1 = bf16[32,16,2048]{2,1,0:T(8,128)(2,1)} custom-call(f32[32]{0:T(128)S(1)} %copy-done.1, bf16[16,2048]{1,0:T(8,128)(2,1)S(1)} %get-tuple-element.10.own_ref, bf16[2,32,2048]{2,1,0:T(8,128)(2,1)S(1)} %bitcast.39), custom_call_target="tpu_custom_call" | custom-call | tf_op jit(solution)/shard_map/backward_planes/pallas_call | solution.py:302
  (15 shorter events, 0.3 us)
Async XLA Ops:
  0.6 0.7 %copy-start = (f32[32]{0:T(128)S(1)}, f32[32]{0:T(128)}, u32[]{:S(2)}) copy-start(f32[32]{0:T(128)} %magnify_ref.1) | copy-start | bytes 388
  1.3 20.1 %copy-start.2 = (f32[16,512]{1,0:T(8,128)S(1)}, f32[16,512]{1,0:T(8,128)}, u32[]{:S(2)}) copy-start(f32[16,512]{1,0:T(8,128)} %param.6) | copy-start | bytes 98308
  1.3 20.2 %copy-start.3 = (s32[16,512]{1,0:T(8,128)S(1)}, s32[16,512]{1,0:T(8,128)}, u32[]{:S(2)}) copy-start(s32[16,512]{1,0:T(8,128)} %param.7) | copy-start | bytes 98308
  8.9 12.6 %collective-permute-start = (bf16[16,2048]{1,0:T(8,128)(2,1)S(1)}, bf16[16,2048]{1,0:T(8,128)(2,1)S(1)}, u32[]{:S(2)}, u32[]{:S(2)}) collective-permute-start(bf16[16,2048]{1,0:T(8,128)(2,1)S(1)} %get-tuple-element.16), channel_id=1, source_target_pairs={{0,4},{2,6},{4,8},{5,1},{6,10},{7,3},{8,12},{9,5},{10,14},{11,7},{... | collective-permute-start | bytes 196616 | tf_op jit(solution)/shard_map/ppermute | solution.py:346
  19.5 5.9 %collective-permute-start.1 = (bf16[16,2048]{1,0:T(8,128)(2,1)S(1)}, bf16[16,2048]{1,0:T(8,128)(2,1)S(1)}, u32[]{:S(2)}, u32[]{:S(2)}) collective-permute-start(bf16[16,2048]{1,0:T(8,128)(2,1)S(1)} %get-tuple-element.17), channel_id=1, source_target_pairs={{0,8},{2,10},{4,12},{6,14},{8,16},{9,1},{10,18},{11,3},{12,20},{13... | collective-permute-start | bytes 196616 | tf_op jit(solution)/shard_map/ppermute | solution.py:346
  38.2 16.9 %copy-start.1 = (f32[32]{0:T(128)S(1)}, f32[32]{0:T(128)}, u32[]{:S(2)}) copy-start(f32[32]{0:T(128)} %magnify_ref.1) | copy-start | bytes 388
  40.4 6.9 %collective-permute-start.3 = (bf16[16,2048]{1,0:T(8,128)(2,1)S(1)}, bf16[16,2048]{1,0:T(8,128)(2,1)S(1)}, u32[]{:S(2)}, u32[]{:S(2)}) collective-permute-start(bf16[16,2048]{1,0:T(8,128)(2,1)S(1)} %get-tuple-element.10.own_ref), channel_id=1, source_target_pairs={{0,8},{2,10},{4,12},{6,14},{8,16},{9,1},{10,18},{11,3},{12,20},{13... | collective-permute-start | bytes 196616 | tf_op jit(solution)/shard_map/ppermute | solution.py:346
  43.8 6.0 %collective-permute-start.2 = (bf16[16,2048]{1,0:T(8,128)(2,1)S(1)}, bf16[16,2048]{1,0:T(8,128)(2,1)S(1)}, u32[]{:S(2)}, u32[]{:S(2)}) collective-permute-start(bf16[16,2048]{1,0:T(8,128)(2,1)S(1)} %get-tuple-element.10.own_ref), channel_id=1, source_target_pairs={{0,4},{2,6},{4,8},{5,1},{6,10},{7,3},{8,12},{9,5},{10,14},{11,7},{... | collective-permute-start | bytes 196616 | tf_op jit(solution)/shard_map/ppermute | solution.py:346
